TPU v7x, 128 devices: a whole 4x4x4 slice. The times are simulated.
128 devices in a mesh: group: 2 (over z_lo), dp: 8 (over z_hi, y), tensor: 8 (over x, core).
Axes of the slice: x: 4, y: 4, z: 4 (z_hi: 2, z_lo: 2; z = z_hi * 2 + z_lo), core: 2. Of those that a mesh axis runs over, the one named last changes fastest.
Arguments:
- context: bfloat16 [1536, 8192], P('dp', ('group', 'tensor')), may hold values from -6 to 6
- low: bfloat16 [1536, 8192], P(('group', 'tensor'), 'dp'), may hold values from -6 to 6
- mid: bfloat16 [1536, 8192], P(('group', 'tensor'), 'dp'), may hold values from -6 to 6
- top: bfloat16 [1536, 8192], P('dp', ('group', 'tensor')), may hold values from -18 to 18
- segments: int32 [1536], replicated, may hold values from 0 to 15, never falling along the last dimension, each value on 1 to 192 neighbouring positions
- output_weight: bfloat16 [8192, 8192], P(('group', 'tensor'), 'dp'), may hold values from -0.0625 to 0.0625
- join_weight: bfloat16 [3, 8192, 8192], P(None, 'dp', ('group', 'tensor')), may hold values from -0.0390625 to 0.0390625
- inner_weight: bfloat16 [8192, 14336], P(('group', 'tensor'), 'dp'), may hold values from -0.0625 to 0.0625
- outer_weight: bfloat16 [14336, 8192], P('dp', ('group', 'tensor')), may hold values from -0.046875 to 0.046875
- norm_gain: float32 [8192], P(('group', 'tensor')), may hold values from 0.25 to 1.75
Outputs:
- mean_error: float32 [], replicated
- grad_join: float32 [3, 8192, 8192], P(None, 'dp', ('group', 'tensor'))
- grad_inner: float32 [8192, 14336], P(('group', 'tensor'), 'dp')
- grad_outer: float32 [14336, 8192], P('dp', ('group', 'tensor'))
Inputs may be any that keep to these rules, and one draw needn't show every extreme that they name: `segments`: segment numbers never fall along the tokens; each document spans 1 to 192 tokens.
All inputs are finite; a program needn't handle non-finite values.
Results may differ from a plain program's by a relative error of at most 0.034.
Values may be sent and summed in bfloat16 or wider, within the bound.
No kernel may reach another device: no remote copies, remote signals or barrier semaphores. Data moves between devices by JAX's collectives and lax.ppermute only.
A program may use at most 192 MiB of HBM per device.

v0:
```python
import math

import jax
import jax.numpy as jnp
from jax import lax
from jax.sharding import PartitionSpec as P

D = 8192
STEPS = 2


epsilon = 1e-05


def shifted(block, axis, distance):
    devices = range(lax.axis_size(axis))
    route = [(i - distance, i) for i in devices if i - distance in devices]
    return lax.ppermute(block, axis, route)


def product(rows, weight, flipped):
    if flipped:
        return lax.dot_general(
            rows, weight, (((1,), (1,)), ((), ())), preferred_element_type=jnp.float32
        )
    return jnp.dot(rows, weight, preferred_element_type=jnp.float32)


def contract_rows(left, right):
    return lax.dot_general(
        left, right, (((0,), (0,)), ((), ())), preferred_element_type=jnp.float32
    )


def gather_rows(values):
    return lax.all_gather(values, "dp", axis=0, tiled=True)


def gather_units(values):
    return lax.all_gather(values, ("group", "tensor"), axis=0, tiled=True)


def row_total(values):
    return lax.psum(values, ("group", "tensor"))


def product_term(gathered, weight, flipped):

    def term(start, count):
        return product(gathered, weight, flipped)

    return term


def high_share(gathered, weight, local_rows):
    return lax.psum_scatter(
        product_term(gathered, weight, False)(
            jnp.int32(0), lax.axis_size(("group", "tensor")) * local_rows
        ).astype(jnp.bfloat16),
        ("group", "tensor"),
        scatter_dimension=0,
        tiled=True,
    ).astype(jnp.float32)


def unit_share(gathered, weight, flipped, local_rows):
    return lax.psum_scatter(
        product_term(gathered, weight, flipped)(
            jnp.int32(0), lax.axis_size(("group", "tensor")) * local_rows
        ).astype(jnp.bfloat16),
        ("group", "tensor"),
        scatter_dimension=0,
        tiled=True,
    ).astype(jnp.float32)


def to_tokens(term, local_rows):
    return lax.psum_scatter(
        term(jnp.int32(0), lax.axis_size("dp") * local_rows).astype(jnp.bfloat16),
        "dp",
        scatter_dimension=0,
        tiled=True,
    ).astype(jnp.float32)


def body(
    context,
    low,
    mid,
    top,
    segments,
    output_weight,
    join_weight,
    inner_weight,
    outer_weight,
    norm_gain,
):
    rows_a = context.shape[0]
    rows_b = low.shape[0]
    tokens = rows_a * lax.axis_size("dp")
    place = lax.axis_index("dp") * rows_a
    context_all = gather_rows(context)
    high = (mid.astype(jnp.float32) + high_share(context_all, output_weight, rows_b)).astype(
        jnp.bfloat16
    )
    hidden_all = (
        lax.all_gather(low, ("group", "tensor"), axis=0, tiled=True),
        lax.all_gather(mid, ("group", "tensor"), axis=0, tiled=True),
        lax.all_gather(high, ("group", "tensor"), axis=0, tiled=True),
    )

    def join_term(start, count):
        total = product(hidden_all[0], join_weight[0], False)
        total = total + product(hidden_all[1], join_weight[1], False)
        return total + product(hidden_all[2], join_weight[2], False)

    state = to_tokens(join_term, rows_a).astype(jnp.bfloat16)
    seg_pad = jnp.concatenate([segments, jnp.full((STEPS + 1,), -1, jnp.int32)])
    seg_window = lax.dynamic_slice_in_dim(seg_pad, place, rows_a + STEPS + 1, 0)
    following_top = shifted(top[: STEPS + 1], "dp", -1)
    top_ext = jnp.concatenate([top, following_top], axis=0).astype(jnp.float32)
    saved = []
    total = jnp.zeros((), jnp.float32)
    for step in range(STEPS):
        xfull = state.astype(jnp.float32)
        sums = row_total(jnp.sum(xfull * xfull, axis=1))
        scale = lax.rsqrt(sums / D + epsilon)[:, None]
        normed = (xfull * scale * norm_gain).astype(jnp.bfloat16)
        normed_all = gather_rows(normed)
        inner = unit_share(normed_all, inner_weight, False, rows_b)
        active = jax.nn.silu(inner).astype(jnp.bfloat16)
        active_all = gather_units(active)
        update = to_tokens(product_term(active_all, outer_weight, False), rows_a)
        following = (xfull + update).astype(jnp.bfloat16)
        valid = (seg_window[step + 1 : step + 1 + rows_a] == seg_window[:rows_a]).astype(
            jnp.float32
        )
        error = valid[:, None] * (
            following.astype(jnp.float32) - top_ext[step + 1 : step + 1 + rows_a]
        )
        total = total + jnp.sum(error * error)
        saved.append((xfull, scale, normed_all, inner, active_all, error))
        state = following
    mean_error = lax.psum(total, ("group", "dp", "tensor")) / (STEPS * tokens * D)
    rate = 1.0 / math.sqrt(tokens)
    grad = jnp.zeros(context.shape, jnp.float32)
    grad_inner = jnp.zeros(inner_weight.shape, jnp.float32)
    grad_outer = jnp.zeros(outer_weight.shape, jnp.float32)
    for step in reversed(range(STEPS)):
        xfull, scale, normed_all, inner, active_all, error = saved[step]
        grad = grad + rate * error
        grad_all = gather_rows(grad.astype(jnp.bfloat16))
        grad_outer = grad_outer + contract_rows(active_all, grad_all)
        back_act = unit_share(grad_all, outer_weight, True, rows_b)
        sigma = jax.nn.sigmoid(inner)
        grad_in = (back_act * sigma * (1.0 + inner * (1.0 - sigma))).astype(jnp.bfloat16)
        grad_in_all = gather_units(grad_in)
        grad_inner = grad_inner + contract_rows(normed_all, grad_in_all)
        back_norm = to_tokens(product_term(grad_in_all, inner_weight, True), rows_a)
        inner_prod = row_total(jnp.sum(back_norm * norm_gain * xfull, axis=1))[:, None]
        grad = grad + scale * norm_gain * back_norm - xfull * scale**3 * inner_prod / D
    grad_all = gather_rows(grad.astype(jnp.bfloat16))
    grad_join = jnp.stack([contract_rows(source, grad_all) for source in hidden_all])
    return (mean_error, grad_join, grad_inner, grad_outer)


def solution(mesh):
    in_specs = (
        P("dp", ("group", "tensor")),
        P(("group", "tensor"), "dp"),
        P(("group", "tensor"), "dp"),
        P("dp", ("group", "tensor")),
        P(),
        P(("group", "tensor"), "dp"),
        P(None, "dp", ("group", "tensor")),
        P(("group", "tensor"), "dp"),
        P("dp", ("group", "tensor")),
        P(("group", "tensor")),
    )
    out_specs = (
        P(),
        P(None, "dp", ("group", "tensor")),
        P(("group", "tensor"), "dp"),
        P("dp", ("group", "tensor")),
    )
    return jax.shard_map(body, mesh=mesh, in_specs=in_specs, out_specs=out_specs, check_vma=False)
```

profile of v0, /device:TPU:1, one launch (start us, length us, event | category | flops | bytes accessed | tf_op | source)
XLA Modules:
  0.0 1560.3 jit_solution(12098348974122804286)
XLA Ops:
  8.0 55.3 %all-gather.18.cloned.1.call-done = bf16[1536,512]{1,0:T(8,128)(2,1)} async-done(((bf16[192,512]{1,0:T(8,128)(2,1)}), bf16[1536,512]{1,0:T(8,128)(2,1)}) %all-gather.18.cloned.1.call-update) | async-done | bytes 1572880 | tf_op jit(solution)/shard_map/all_gather | solution.py:36
  69.9 60.2 %reduce-scatter.11.cloned.1.call-done = bf16[96,1024]{1,0:T(8,128)(2,1)} async-done(((bf16[1536,1024]{1,0:T(8,128)(2,1)}), bf16[96,1024]{1,0:T(8,128)(2,1)}) %reduce-scatter.11.cloned.1.call-update) | async-done | bytes 196624 | tf_op jit(solution)/shard_map/reduce_scatter | solution.py:56
  131.8 38.5 %all-gather.14.cloned.1.call-done = bf16[1536,1024]{1,0:T(8,128)(2,1)} async-done(((bf16[96,1024]{1,0:T(8,128)(2,1)}), bf16[1536,1024]{1,0:T(8,128)(2,1)}) %all-gather.14.cloned.1.call-update) | async-done | bytes 3145744 | tf_op jit(solution)/shard_map/all_gather | solution.py:107
  176.0 31.9 %all-gather.16.cloned.1.call-done = bf16[1536,1024]{1,0:T(8,128)(2,1)} async-done(((bf16[96,1024]{1,0:T(8,128)(2,1)}), bf16[1536,1024]{1,0:T(8,128)(2,1)}) %all-gather.16.cloned.1.call-update) | async-done | bytes 3145744 | tf_op jit(solution)/shard_map/all_gather | solution.py:108
  214.5 31.5 %all-gather.20.cloned.1.call-done = bf16[1536,1024]{1,0:T(8,128)(2,1)} async-done(((bf16[96,1024]{1,0:T(8,128)(2,1)}), bf16[1536,1024]{1,0:T(8,128)(2,1)}) %all-gather.20.cloned.1.call-update) | async-done | bytes 3145744 | tf_op jit(solution)/shard_map/all_gather | solution.py:109
  252.2 73.2 %reduce-scatter.13.cloned.1.call-done = bf16[192,512]{1,0:T(8,128)(2,1)} async-done(((bf16[1536,512]{1,0:T(8,128)(2,1)}), bf16[192,512]{1,0:T(8,128)(2,1)}) %reduce-scatter.13.cloned.1.call-update) | async-done | bytes 196624 | tf_op jit(solution)/shard_map/reduce_scatter | solution.py:78
  326.4 28.3 %psum.35 = f32[192]{0:T(256)S(1)} all-reduce(f32[192]{0:T(256)S(1)} %fusion.28), channel_id=1, replica_groups=mesh['group'=2,'dp'=8,'tensor'=8] {'group','tensor'}, use_global_device_ids=true, to_apply=%region_3.0 | all-reduce | flops 192 | bytes 1536 | tf_op jit(solution)/shard_map/psum | solution.py:44
  356.5 47.9 %all-gather.22.cloned.1.call-done = bf16[1536,512]{1,0:T(8,128)(2,1)} async-done(((bf16[192,512]{1,0:T(8,128)(2,1)}), bf16[1536,512]{1,0:T(8,128)(2,1)}) %all-gather.22.cloned.1.call-update) | async-done | bytes 1572880 | tf_op jit(solution)/shard_map/all_gather | solution.py:36
  412.0 65.6 %reduce-scatter.15.cloned.1.call-done = bf16[96,1792]{1,0:T(8,128)(2,1)} async-done(((bf16[1536,1792]{1,0:T(8,128)(2,1)}), bf16[96,1792]{1,0:T(8,128)(2,1)}) %reduce-scatter.15.cloned.1.call-update) | async-done | bytes 344080 | tf_op jit(solution)/shard_map/reduce_scatter | solution.py:67
  479.5 43.6 %all-gather.24.cloned.1.call-done = bf16[1536,1792]{1,0:T(8,128)(2,1)} async-done(((bf16[96,1792]{1,0:T(8,128)(2,1)}), bf16[1536,1792]{1,0:T(8,128)(2,1)}) %all-gather.24.cloned.1.call-update) | async-done | bytes 5505040 | tf_op jit(solution)/shard_map/all_gather | solution.py:40
  529.8 72.9 %reduce-scatter.17.cloned.1.call-done = bf16[192,512]{1,0:T(8,128)(2,1)} async-done(((bf16[1536,512]{1,0:T(8,128)(2,1)}), bf16[192,512]{1,0:T(8,128)(2,1)}) %reduce-scatter.17.cloned.1.call-update) | async-done | bytes 196624 | tf_op jit(solution)/shard_map/reduce_scatter | solution.py:78
  633.4 47.4 %all-gather.26.cloned.1.call-done = bf16[1536,512]{1,0:T(8,128)(2,1)} async-done(((bf16[192,512]{1,0:T(8,128)(2,1)}), bf16[1536,512]{1,0:T(8,128)(2,1)}) %all-gather.26.cloned.1.call-update) | async-done | bytes 1572880 | tf_op jit(solution)/shard_map/all_gather | solution.py:36
  688.4 65.6 %reduce-scatter.19.cloned.1.call-done = bf16[96,1792]{1,0:T(8,128)(2,1)} async-done(((bf16[1536,1792]{1,0:T(8,128)(2,1)}), bf16[96,1792]{1,0:T(8,128)(2,1)}) %reduce-scatter.19.cloned.1.call-update) | async-done | bytes 344080 | tf_op jit(solution)/shard_map/reduce_scatter | solution.py:67
  756.0 43.4 %all-gather.28.cloned.1.call-done = bf16[1536,1792]{1,0:T(8,128)(2,1)} async-done(((bf16[96,1792]{1,0:T(8,128)(2,1)}), bf16[1536,1792]{1,0:T(8,128)(2,1)}) %all-gather.28.cloned.1.call-update) | async-done | bytes 5505040 | tf_op jit(solution)/shard_map/all_gather | solution.py:40
  810.5 68.5 %reduce-scatter.21.cloned.1.call-done = bf16[192,512]{1,0:T(8,128)(2,1)} async-done(((bf16[1536,512]{1,0:T(8,128)(2,1)}), bf16[192,512]{1,0:T(8,128)(2,1)}) %reduce-scatter.21.cloned.1.call-update) | async-done | bytes 196624 | tf_op jit(solution)/shard_map/reduce_scatter | solution.py:78
  880.9 50.5 %all-gather.30.cloned.1.call-done = bf16[1536,512]{1,0:T(8,128)(2,1)} async-done(((bf16[192,512]{1,0:T(8,128)(2,1)}), bf16[1536,512]{1,0:T(8,128)(2,1)}) %all-gather.30.cloned.1.call-update) | async-done | bytes 1572880 | tf_op jit(solution)/shard_map/all_gather | solution.py:36
  938.0 65.6 %reduce-scatter.23.cloned.1.call-done = bf16[96,1792]{1,0:T(8,128)(2,1)} async-done(((bf16[1536,1792]{1,0:T(8,128)(2,1)}), bf16[96,1792]{1,0:T(8,128)(2,1)}) %reduce-scatter.23.cloned.1.call-update) | async-done | bytes 344080 | tf_op jit(solution)/shard_map/reduce_scatter | solution.py:67
  1005.7 43.3 %all-gather.32.cloned.1.call-done = bf16[1536,1792]{1,0:T(8,128)(2,1)} async-done(((bf16[96,1792]{1,0:T(8,128)(2,1)}), bf16[1536,1792]{1,0:T(8,128)(2,1)}) %all-gather.32.cloned.1.call-update) | async-done | bytes 5505040 | tf_op jit(solution)/shard_map/all_gather | solution.py:40
  1056.4 72.9 %reduce-scatter.25.cloned.1.call-done = bf16[192,512]{1,0:T(8,128)(2,1)} async-done(((bf16[1536,512]{1,0:T(8,128)(2,1)}), bf16[192,512]{1,0:T(8,128)(2,1)}) %reduce-scatter.25.cloned.1.call-update) | async-done | bytes 196624 | tf_op jit(solution)/shard_map/reduce_scatter | solution.py:78
  1161.3 47.9 %all-gather.34.cloned.1.call-done = bf16[1536,512]{1,0:T(8,128)(2,1)} async-done(((bf16[192,512]{1,0:T(8,128)(2,1)}), bf16[1536,512]{1,0:T(8,128)(2,1)}) %all-gather.34.cloned.1.call-update) | async-done | bytes 1572880 | tf_op jit(solution)/shard_map/all_gather | solution.py:36
  1215.9 65.6 %reduce-scatter.27.cloned.1.call-done = bf16[96,1792]{1,0:T(8,128)(2,1)} async-done(((bf16[1536,1792]{1,0:T(8,128)(2,1)}), bf16[96,1792]{1,0:T(8,128)(2,1)}) %reduce-scatter.27.cloned.1.call-update) | async-done | bytes 344080 | tf_op jit(solution)/shard_map/reduce_scatter | solution.py:67
  1283.8 43.2 %all-gather.36.cloned.1.call-done = bf16[1536,1792]{1,0:T(8,128)(2,1)} async-done(((bf16[96,1792]{1,0:T(8,128)(2,1)}), bf16[1536,1792]{1,0:T(8,128)(2,1)}) %all-gather.36.cloned.1.call-update) | async-done | bytes 5505040 | tf_op jit(solution)/shard_map/all_gather | solution.py:40
  1333.8 73.0 %reduce-scatter.29.cloned.1.call-done = bf16[192,512]{1,0:T(8,128)(2,1)} async-done(((bf16[1536,512]{1,0:T(8,128)(2,1)}), bf16[192,512]{1,0:T(8,128)(2,1)}) %reduce-scatter.29.cloned.1.call-update) | async-done | bytes 196624 | tf_op jit(solution)/shard_map/reduce_scatter | solution.py:78
  1454.8 64.9 %psum.37 = f32[]{:T(128)} all-reduce(f32[]{:T(128)S(6)} %add.99), channel_id=1, replica_groups=mesh['group'=2,'dp'=8,'tensor'=8] {'group','dp','tensor'}, use_global_device_ids=true, to_apply=%region_12.13 | all-reduce | flops 1 | bytes 8 | tf_op jit(solution)/shard_map/psum | solution.py:144
  (132 shorter events, 242.0 us)
Async XLA Ops:
  7.2 56.1 %all-gather.18.cloned.1.call-start = ((), (), s32[]{:S(2)}) async-start(), calls=%async_computation.12 | async-start | bytes 1769472 | tf_op jit(solution)/shard_map/all_gather | solution.py:36
  7.9 122.1 %reduce-scatter.11.cloned.1.call-start = ((), (), s32[]{:S(2)}) async-start(), calls=%async_computation.13 | async-start | bytes 3342336 | tf_op jit(solution)/shard_map/reduce_scatter | solution.py:56
  68.5 101.8 %all-gather.14.cloned.1.call-start = ((), (), s32[]{:S(2)}) async-start(), calls=%async_computation.10 | async-start | bytes 3342336 | tf_op jit(solution)/shard_map/all_gather | solution.py:107
  69.2 138.6 %all-gather.16.cloned.1.call-start = ((), (), s32[]{:S(2)}) async-start(), calls=%async_computation.11 | async-start | bytes 3342336 | tf_op jit(solution)/shard_map/all_gather | solution.py:108
  69.8 176.2 %all-gather.20.cloned.1.call-start = ((), (), s32[]{:S(2)}) async-start(), calls=%async_computation.14 | async-start | bytes 3342336 | tf_op jit(solution)/shard_map/all_gather | solution.py:109
  131.7 193.7 %reduce-scatter.13.cloned.1.call-start = ((), (), s32[]{:S(2)}) async-start(), calls=%async_computation.15 | async-start | bytes 1769472 | tf_op jit(solution)/shard_map/reduce_scatter | solution.py:78
  252.1 152.3 %all-gather.22.cloned.1.call-start = ((), (), s32[]{:S(2)}) async-start(), calls=%async_computation.16 | async-start | bytes 1769472 | tf_op jit(solution)/shard_map/all_gather | solution.py:36
  356.5 121.0 %reduce-scatter.15.cloned.1.call-start = ((), (), s32[]{:S(2)}) async-start(), calls=%async_computation.17 | async-start | bytes 5849088 | tf_op jit(solution)/shard_map/reduce_scatter | solution.py:67
  411.9 111.2 %all-gather.24.cloned.1.call-start = ((), (), s32[]{:S(2)}) async-start(), calls=%async_computation.18 | async-start | bytes 5849088 | tf_op jit(solution)/shard_map/all_gather | solution.py:40
  479.5 123.3 %reduce-scatter.17.cloned.1.call-start = ((), (), s32[]{:S(2)}) async-start(), calls=%async_computation.19 | async-start | bytes 1769472 | tf_op jit(solution)/shard_map/reduce_scatter | solution.py:78
  529.8 151.1 %all-gather.26.cloned.1.call-start = ((), (), s32[]{:S(2)}) async-start(), calls=%async_computation.20 | async-start | bytes 1769472 | tf_op jit(solution)/shard_map/all_gather | solution.py:36
  632.9 121.1 %reduce-scatter.19.cloned.1.call-start = ((), (), s32[]{:S(2)}) async-start(), calls=%async_computation.21 | async-start | bytes 5849088 | tf_op jit(solution)/shard_map/reduce_scatter | solution.py:67
  688.3 111.1 %all-gather.28.cloned.1.call-start = ((), (), s32[]{:S(2)}) async-start(), calls=%async_computation.22 | async-start | bytes 5849088 | tf_op jit(solution)/shard_map/all_gather | solution.py:40
  755.9 123.2 %reduce-scatter.21.cloned.1.call-start = ((), (), s32[]{:S(2)}) async-start(), calls=%async_computation.23 | async-start | bytes 1769472 | tf_op jit(solution)/shard_map/reduce_scatter | solution.py:78
  806.1 125.2 %all-gather.30.cloned.1.call-start = ((), (), s32[]{:S(2)}) async-start(), calls=%async_computation.24 | async-start | bytes 1769472 | tf_op jit(solution)/shard_map/all_gather | solution.py:36
  806.1 4.4 collective-permute-start
  880.8 122.8 %reduce-scatter.23.cloned.1.call-start = ((), (), s32[]{:S(2)}) async-start(), calls=%async_computation.25 | async-start | bytes 5849088 | tf_op jit(solution)/shard_map/reduce_scatter | solution.py:67
  938.0 111.0 %all-gather.32.cloned.1.call-start = ((), (), s32[]{:S(2)}) async-start(), calls=%async_computation.26 | async-start | bytes 5849088 | tf_op jit(solution)/shard_map/all_gather | solution.py:40
  1005.6 123.7 %reduce-scatter.25.cloned.1.call-start = ((), (), s32[]{:S(2)}) async-start(), calls=%async_computation.27 | async-start | bytes 1769472 | tf_op jit(solution)/shard_map/reduce_scatter | solution.py:78
  1056.3 152.9 %all-gather.34.cloned.1.call-start = ((), (), s32[]{:S(2)}) async-start(), calls=%async_computation.28 | async-start | bytes 1769472 | tf_op jit(solution)/shard_map/all_gather | solution.py:36
  1161.3 120.3 %reduce-scatter.27.cloned.1.call-start = ((), (), s32[]{:S(2)}) async-start(), calls=%async_computation.29 | async-start | bytes 5849088 | tf_op jit(solution)/shard_map/reduce_scatter | solution.py:67
  1215.9 111.1 %all-gather.36.cloned.1.call-start = ((), (), s32[]{:S(2)}) async-start(), calls=%async_computation.30 | async-start | bytes 5849088 | tf_op jit(solution)/shard_map/all_gather | solution.py:40
  1283.6 123.2 %reduce-scatter.29.cloned.1.call-start = ((), (), s32[]{:S(2)}) async-start(), calls=%async_computation.31 | async-start | bytes 1769472 | tf_op jit(solution)/shard_map/reduce_scatter | solution.py:78
  1333.7 200.7 %all-gather.38.cloned.1.call-start = ((), (), s32[]{:S(2)}) async-start(), calls=%async_computation.32 | async-start | bytes 1769472 | tf_op jit(solution)/shard_map/all_gather | solution.py:36
  (19 other events, 1445.3 us)
Sparse Core Ops, SparseCore 0:
  10.3 52.9 all-gather.17
  68.6 61.3 reduce-scatter.10
  131.8 38.5 all-gather.13
  171.9 35.9 all-gather.15
  210.0 35.9 all-gather.19
  252.2 73.1 reduce-scatter.12
  356.6 47.7 all-gather.21
  412.0 65.4 reduce-scatter.14
  479.9 43.1 all-gather.23
  529.9 72.7 reduce-scatter.16
  633.0 47.7 all-gather.25
  688.4 65.4 reduce-scatter.18
  756.2 43.1 all-gather.27
  806.2 72.8 reduce-scatter.20
  881.8 49.4 all-gather.29
  938.1 65.4 reduce-scatter.22
  1005.8 43.0 all-gather.31
  1056.5 72.8 reduce-scatter.24
  1161.4 47.7 all-gather.33
  1216.0 65.4 reduce-scatter.26
  1283.8 43.0 all-gather.35
  1333.8 72.8 reduce-scatter.28
  1438.0 48.0 all-gather.37
where the time goes:
time: 1570 us; the launch traced here: 1560 us
  waiting for transfers between devices  1210 us (77%)
  blocking collectives  178 us (11%)
  matrix products  117 us (7%)
  other arithmetic  25.7 us (2%)
  between operations  17.6 us (1%)
    reduce_scatter x5, waiting for transfers between devices, to_tokens(): lax.psum_scatter(term(jnp.int32(0), lax.axis_size('dp') * local_rows).ast...  361 us
    reduce_scatter x4, waiting for transfers between devices, unit_share(): lax.psum_scatter(product_term(gathered, weight, flipped)(jnp.int32(0), la...  262 us
    all_gather x6, waiting for transfers between devices, gather_rows(): return lax.all_gather(values, 'dp', axis=0, tiled=True)  249 us
    all_gather x4, waiting for transfers between devices, gather_units(): return lax.all_gather(values, ('group', 'tensor'), axis=0, tiled=True)  173 us
    psum x4, blocking collectives, row_total(): return lax.psum(values, ('group', 'tensor'))  113 us
    psum x1, blocking collectives, body(): lax.psum(total, ('group', 'dp', 'tensor')) / (STEPS * tokens * D)  64.9 us
    reduce_scatter x1, waiting for transfers between devices, high_share(): lax.psum_scatter(product_term(gathered, weight, False)(jnp.int32(0), lax....  60.2 us
    dot_general x8, matrix products, product(): return jnp.dot(rows, weight, preferred_element_type=jnp.float32)  51.7 us
  transfers between devices with their start and end apart: 24, of which 23 were waited for; matrix products, arithmetic and copies ran while one was open for 3% of the time, Pallas kernels for 0%

commit v1 on v0

v1 whole, which is shorter than its diff:
```python
import math

import jax
import jax.numpy as jnp
from jax import lax
from jax.sharding import PartitionSpec as P

D = 8192
STEPS = 2
epsilon = 1e-05

F32 = jnp.float32
BF16 = jnp.bfloat16
UNITS = ("group", "tensor")
EVERY = ("group", "dp", "tensor")


def chip_peers():
    n = lax.axis_size(UNITS)
    return [[chip * 2 + core for chip in range(n // 2)] for core in range(2)]


def other_core(values):
    n = lax.axis_size("tensor")
    return lax.ppermute(values, "tensor", [(i, i ^ 1) for i in range(n)])


def other_group(values):
    return lax.ppermute(values, "group", [(0, 1), (1, 0)])


def swap_axes(values):
    groups, n = lax.axis_size("group"), lax.axis_size("dp")
    route = [
        ((k * n + a) * n + b, (k * n + b) * n + a)
        for k in range(groups)
        for a in range(n)
        for b in range(n)
    ]
    return lax.ppermute(values, EVERY, route)


def shifted(block, axis, distance):
    devices = range(lax.axis_size(axis))
    route = [(i - distance, i) for i in devices if i - distance in devices]
    return lax.ppermute(block, axis, route)


def copies(values, axis, count, groups=None):
    sent = jnp.broadcast_to(values[None], (count,) + values.shape)
    return lax.all_to_all(sent, axis, 0, 0, tiled=True, axis_index_groups=groups)


def total_of(blocks, axis, groups=None):
    got = lax.all_to_all(blocks, axis, 0, 0, tiled=True, axis_index_groups=groups)
    return jnp.sum(got.astype(F32), axis=0)


def contract_rows(left, right):
    return lax.dot_general(left, right, (((0,), (0,)), ((), ())), preferred_element_type=F32)


def to_feature_owners(blocks):
    return lax.all_to_all(blocks, "tensor", 0, 0, tiled=True)


def row_gather(values, axis):
    block = lax.optimization_barrier(jnp.broadcast_to(values[None], (64, values.shape[0])))
    got = lax.optimization_barrier(lax.all_gather(block, axis, axis=0, tiled=True))
    return got.reshape((lax.axis_size(axis), 64, values.shape[0]))[:, :1]


def after(values, *earlier):
    for other in earlier:
        values = values + (0.0 * other.reshape(-1)[0].astype(F32)).astype(values.dtype)
    return values


def body(
    context,
    low,
    mid,
    top,
    segments,
    output_weight,
    join_weight,
    inner_weight,
    outer_weight,
    norm_gain,
):
    n_dp = lax.axis_size("dp")
    n_tensor = lax.axis_size("tensor")
    chips = lax.axis_size(UNITS) // 2
    rows, width = context.shape
    rows_b, width_b = low.shape
    tokens = rows * n_dp
    core = lax.axis_index("tensor") % 2
    peers = chip_peers()
    place = lax.axis_index("tensor") * rows

    own_top = swap_axes(top)
    gains = row_gather(norm_gain, "tensor")
    gain = lax.dynamic_index_in_dim(gains, lax.axis_index("dp"), 0, keepdims=False)
    following_top = shifted(own_top[: STEPS + 1], "tensor", -1)
    top_ext = jnp.concatenate([own_top, following_top], axis=0).astype(F32)
    seg_pad = jnp.concatenate([segments, jnp.full((STEPS + 1,), -1, jnp.int32)])
    seg_window = lax.dynamic_slice_in_dim(seg_pad, place, rows + STEPS + 1, 0)

    low_mid = lax.all_gather(jnp.stack([low, mid]), UNITS, axis=1, tiled=True)
    inner_all = lax.all_gather(inner_weight, "tensor", axis=0, tiled=True).reshape(
        n_tensor, width, -1
    )
    outer_all = lax.all_gather(outer_weight, "tensor", axis=0, tiled=False)

    context_all = copies(context, "dp", n_dp).reshape(tokens, width)
    part = jnp.dot(context_all, output_weight, preferred_element_type=F32).astype(BF16)
    part = part.reshape(chips, 2, rows_b, width_b)
    kept = lax.dynamic_index_in_dim(part, core, 1, keepdims=False)
    given = lax.dynamic_index_in_dim(part, 1 - core, 1, keepdims=False)
    part = (kept.astype(F32) + other_core(given).astype(F32)).astype(BF16)
    high = after(mid.astype(F32), following_top) + total_of(part, UNITS, peers)
    high = high.astype(BF16)
    high_own = copies(high, UNITS, chips, peers)
    high_other = other_core(high_own)
    high_all = jnp.where(
        core == 0,
        jnp.stack([high_own, high_other], axis=1),
        jnp.stack([high_other, high_own], axis=1),
    ).reshape(tokens, width_b)
    hidden_all = (low_mid[0], low_mid[1], high_all)

    joined = jnp.dot(hidden_all[0], join_weight[0], preferred_element_type=F32)
    joined = joined + jnp.dot(hidden_all[1], join_weight[1], preferred_element_type=F32)
    joined = joined + jnp.dot(hidden_all[2], join_weight[2], preferred_element_type=F32)
    joined = total_of(joined.astype(BF16).reshape(n_dp, rows, width), "dp")
    state = swap_axes(joined.astype(BF16))

    saved = []
    total = jnp.zeros((), F32)
    for step in range(STEPS):
        xfull = state.astype(F32)
        x_all = copies(state, "dp", n_dp).astype(F32)
        sums = jnp.sum(x_all * x_all, axis=(0, 2))
        sums = sums + other_group(sums)
        scale = lax.rsqrt(sums / D + epsilon)[:, None]
        normed = (x_all * scale * gains).astype(BF16)
        part = jnp.einsum("brf,bfu->ru", normed, inner_all, preferred_element_type=F32)
        inner = part + other_group(part.astype(BF16)).astype(F32)
        active = jax.nn.silu(inner).astype(BF16)
        update = jnp.einsum("ru,buf->brf", active, outer_all, preferred_element_type=F32)
        update = total_of(update.astype(BF16), "dp")
        following = (xfull + update).astype(BF16)
        valid = (seg_window[step + 1 : step + 1 + rows] == seg_window[:rows]).astype(F32)
        error = valid[:, None] * (following.astype(F32) - top_ext[step + 1 : step + 1 + rows])
        total = total + jnp.sum(error * error)
        active_all = lax.all_gather(active, "tensor", axis=0, tiled=True)
        saved.append((xfull, scale, normed, inner, active_all, error))
        state = following
    rate = 1.0 / math.sqrt(tokens)
    grad = jnp.zeros((rows, width), F32)
    grad_inner = jnp.zeros(inner_weight.shape, F32)
    grad_outer = jnp.zeros(outer_weight.shape, F32)
    for step in reversed(range(STEPS)):
        xfull, scale, normed, inner, active_all, error = saved[step]
        grad = grad + rate * error
        grad_all = copies(grad.astype(BF16), "dp", n_dp)
        part = jnp.einsum("brf,buf->ru", grad_all, outer_all, preferred_element_type=F32)
        back_act = part + other_group(part.astype(BF16)).astype(F32)
        sigma = jax.nn.sigmoid(inner)
        grad_in = (back_act * sigma * (1.0 + inner * (1.0 - sigma))).astype(BF16)
        moved = jnp.sum(grad_in.astype(F32) * inner, axis=1)
        moved = jnp.concatenate([moved, jnp.full((64,), total)]).reshape(2, 128)
        moved = jnp.sum(copies(moved, "dp", n_dp), axis=0).reshape(256)
        total_dp = moved[rows:]
        moved = moved[:rows, None]
        back = jnp.einsum("ru,bfu->brf", grad_in, inner_all, preferred_element_type=F32)
        back_norm = total_of(back.astype(BF16), "dp")
        grad = grad + scale * gain * back_norm - xfull * scale**2 * moved / D
        grad_in_all = lax.all_gather(grad_in, "tensor", axis=0, tiled=True)
        grad_tokens = to_feature_owners(grad_all).reshape(tokens, width)
        grad_outer = grad_outer + contract_rows(active_all, grad_tokens)
        normed_all = to_feature_owners(normed).reshape(tokens, width)
        grad_inner = grad_inner + contract_rows(normed_all, grad_in_all)
    for k in (1, 2, 4):
        total_dp = total_dp + lax.ppermute(
            total_dp, "tensor", [(i, i ^ k) for i in range(n_tensor)]
        )
    mean_error = (total_dp + other_group(total_dp))[0] / (STEPS * tokens * D)
    grad_tokens = copies(swap_axes(grad.astype(BF16)), "dp", n_dp).reshape(tokens, width)
    grad_join = jnp.stack([contract_rows(source, grad_tokens) for source in hidden_all])
    return (mean_error, grad_join, grad_inner, grad_outer)


def solution(mesh):
    in_specs = (
        P("dp", ("group", "tensor")),
        P(("group", "tensor"), "dp"),
        P(("group", "tensor"), "dp"),
        P("dp", ("group", "tensor")),
        P(),
        P(("group", "tensor"), "dp"),
        P(None, "dp", ("group", "tensor")),
        P(("group", "tensor"), "dp"),
        P("dp", ("group", "tensor")),
        P(("group", "tensor")),
    )
    out_specs = (
        P(),
        P(None, "dp", ("group", "tensor")),
        P(("group", "tensor"), "dp"),
        P("dp", ("group", "tensor")),
    )
    return jax.shard_map(body, mesh=mesh, in_specs=in_specs, out_specs=out_specs, check_vma=False)
```

time: 1570 us -> 748 us (0.48)
  waiting for transfers between devices: 1210 us -> 238 us
  starting transfers between devices: 2.88 us -> 99.2 us
  blocking collectives: 178 us -> 210 us
  matrix products: 117 us -> 134 us
    reduce_scatter x10 -> x0, waiting for transfers between devices: 683 us -> none  [the longest x5 361 us: to_tokens(): lax.psum_scatter(term(jnp.int32(0), lax.axis_size('dp') * local_rows).ast...]
    all_gather x13 -> x8, waiting for transfers between devices: 524 us -> 40.1 us  [the longest x1 40 us: body(): outer_all = lax.all_gather(outer_weight, 'tensor', axis=0, tiled=False)]
    all_to_all x0 -> x8, blocking collectives: none -> 210 us  [the longest x5 132 us: copies(): lax.all_to_all(sent, axis, 0, 0, tiled=True, axis_index_groups=groups)]
    psum x5 -> x0, blocking collectives: 178 us -> none  [the longest x4 113 us: row_total(): return lax.psum(values, ('group', 'tensor'))]
    all_to_all x0 -> x11, waiting for transfers between devices: none -> 106 us  [the longest x4 42.2 us: to_feature_owners(): return lax.all_to_all(blocks, 'tensor', 0, 0, tiled=True)]
    all_to_all x0 -> x11, starting transfers between devices: none -> 79.9 us  [the longest x4 31.6 us: to_feature_owners(): return lax.all_to_all(blocks, 'tensor', 0, 0, tiled=True)]
    ppermute x0 -> x15, waiting for transfers between devices: none -> 64.5 us  [the longest x7 41.2 us: other_group(): return lax.ppermute(values, 'group', [(0, 1), (1, 0)])]
    ppermute x1, waiting for transfers between devices: 2.88 us -> 25 us  [shifted(): return lax.ppermute(block, axis, route)]
  transfers between devices with their start and end apart: 24 -> 35, of which waited for: 23 -> 23; matrix products, arithmetic and copies ran while one was open for 3% -> 19% of each run, Pallas kernels for 0% -> 0%
where the time goes in v1:
time: 748 us; the launch traced here: 736 us
  waiting for transfers between devices  238 us (32%)
  blocking collectives  210 us (28%)
  matrix products  134 us (18%)
  starting transfers between devices  99.2 us (13%)
  other arithmetic  26.5 us (4%)
  between operations  18.2 us (2%)
  local copies, waits for them, and re-layouts  10.6 us (1%)
    all_to_all x5, blocking collectives, copies(): lax.all_to_all(sent, axis, 0, 0, tiled=True, axis_index_groups=groups)  132 us
    all_to_all x3, blocking collectives, total_of(): lax.all_to_all(blocks, axis, 0, 0, tiled=True, axis_index_groups=groups)  77.2 us
    dot_general x7, matrix products, contract_rows(): lax.dot_general(left, right, (((0,), (0,)), ((), ())), preferred_element_...  46.9 us
    all_to_all x4, waiting for transfers between devices, to_feature_owners(): return lax.all_to_all(blocks, 'tensor', 0, 0, tiled=True)  42.2 us
    ppermute x7, waiting for transfers between devices, other_group(): return lax.ppermute(values, 'group', [(0, 1), (1, 0)])  41.2 us
    all_gather x1, waiting for transfers between devices, body(): outer_all = lax.all_gather(outer_weight, 'tensor', axis=0, tiled=False)  40 us
    all_to_all x3, waiting for transfers between devices, total_of(): lax.all_to_all(blocks, axis, 0, 0, tiled=True, axis_index_groups=groups)  37.5 us
    all_to_all x4, starting transfers between devices, to_feature_owners(): return lax.all_to_all(blocks, 'tensor', 0, 0, tiled=True)  31.6 us
  transfers between devices with their start and end apart: 35, of which 23 were waited for; matrix products, arithmetic and copies ran while one was open for 19% of the time, Pallas kernels for 0%

profile of v1, /device:TPU:1, one launch (start us, length us, event | category | flops | bytes accessed | tf_op | source)
XLA Modules:
  0.0 735.8 jit_solution(13160684440190373415)
XLA Ops:
  21.5 23.7 %all-to-all-done = bf16[8,192,512]{2,1,0:T(8,128)(2,1)S(1)} async-done(((bf16[8,192,512]{2,1,0:T(8,128)(2,1)}), bf16[8,192,512]{2,1,0:T(8,128)(2,1)S(1)}, u32[]{:S(2)}, u32[]{:S(2)}) %all-to-all-start) | async-done | bytes 1572896 | tf_op jit(solution)/shard_map/all_to_all | solution.py:51
  72.3 25.0 %collective-permute-done.1 = bf16[3,512]{1,0:T(4,128)(2,1)S(1)} collective-permute-done((bf16[3,512]{1,0:T(4,128)(2,1)S(1)}, bf16[3,512]{1,0:T(4,128)(2,1)S(1)}, u32[]{:S(2)}, u32[]{:S(2)}) %collective-permute-start.1) | collective-permute-done | bytes 3104 | tf_op jit(solution)/shard_map/ppermute | solution.py:46
  99.0 30.9 %all_to_all.95 = bf16[8,96,1024]{2,1,0:T(8,128)(2,1)S(1)} all-to-all(bf16[8,96,1024]{2,1,0:T(8,128)(2,1)S(1)} %broadcast_in_dim.25), channel_id=1, replica_groups={{0,2,4,6,64,66,68,70},{1,3,5,7,65,67,69,71},{8,10,12,14,72,74,76,78},{9..., dimensions={0} | all-to-all | bytes 3145728 | tf_op jit(solution)/shard_map/all_to_all | solution.py:51
  146.9 29.0 %all_to_all.96 = bf16[8,192,512]{2,1,0:T(8,128)(2,1)S(1)} all-to-all(bf16[8,192,512]{2,1,0:T(8,128)(2,1)S(1)} %bitcast.128), channel_id=1, replica_groups=mesh['group'=2,'dp'=8,'tensor'=8] {'dp'}, dimensions={0} | all-to-all | bytes 3145728 | tf_op jit(solution)/shard_map/all_to_all | solution.py:55
  185.3 35.8 %all_to_all.97 = bf16[8,192,512]{2,1,0:T(8,128)(2,1)S(1)} all-to-all(bf16[8,192,512]{2,1,0:T(8,128)(2,1)S(1)} %broadcast_in_dim.26), channel_id=1, replica_groups=mesh['group'=2,'dp'=8,'tensor'=8] {'dp'}, dimensions={0} | all-to-all | bytes 3145728 | tf_op jit(solution)/shard_map/all_to_all | solution.py:51
  233.8 12.3 %collective-permute-done.6 = bf16[192,1792]{1,0:T(8,128)(2,1)S(1)} collective-permute-done((bf16[192,1792]{1,0:T(8,128)(2,1)S(1)}, bf16[192,1792]{1,0:T(8,128)(2,1)S(1)}, u32[]{:S(2)}, u32[]{:S(2)}) %collective-permute-start.6) | collective-permute-done | bytes 688160 | tf_op jit(solution)/shard_map/ppermute | solution.py:29
  246.5 40.0 %all-gather.24.cloned.1.call-done = bf16[14336,512]{1,0:T(8,128)(2,1)} async-done(((bf16[1792,512]{1,0:T(8,128)(2,1)}), bf16[14336,512]{1,0:T(8,128)(2,1)}) %all-gather.24.cloned.1.call-update) | async-done | bytes 14680080 | tf_op jit(solution)/shard_map/all_gather | solution.py:113
  286.5 9.3 %fusion.13 = bf16[8,192,512]{2,1,0:T(8,128)(2,1)} fusion(bf16[8,1792,512]{2,1,0:T(8,128)(2,1)} %bitcast.144, bf16[192,1792]{1,0:T(8,128)(2,1)S(1)} %multiply_convert_fusion.3), kind=kOutput, calls=%fused_computation.42 | convolution fusion | flops 2819358720 | bytes 16941056 | tf_op jit(solution)/shard_map/ru,buf->brf/dot_general | solution.py:150
  302.9 22.7 %all-to-all-done.5 = bf16[8,192,512]{2,1,0:T(8,128)(2,1)S(1)} async-done(((bf16[8,192,512]{2,1,0:T(8,128)(2,1)}), bf16[8,192,512]{2,1,0:T(8,128)(2,1)S(1)}, u32[]{:S(2)}, u32[]{:S(2)}) %all-to-all-start.5) | async-done | bytes 1572896 | tf_op jit(solution)/shard_map/all_to_all | solution.py:55
  326.7 24.7 %all_to_all.98 = bf16[8,192,512]{2,1,0:T(8,128)(2,1)S(1)} all-to-all(bf16[8,192,512]{2,1,0:T(8,128)(2,1)S(1)} %broadcast_in_dim.28), channel_id=1, replica_groups=mesh['group'=2,'dp'=8,'tensor'=8] {'dp'}, dimensions={0} | all-to-all | bytes 3145728 | tf_op jit(solution)/shard_map/all_to_all | solution.py:51
  363.8 13.1 %collective-permute-done.8 = bf16[192,1792]{1,0:T(8,128)(2,1)S(1)} collective-permute-done((bf16[192,1792]{1,0:T(8,128)(2,1)S(1)}, bf16[192,1792]{1,0:T(8,128)(2,1)S(1)}, u32[]{:S(2)}, u32[]{:S(2)}) %collective-permute-start.8) | collective-permute-done | bytes 688160 | tf_op jit(solution)/shard_map/ppermute | solution.py:29
  387.2 21.2 %all_to_all.99 = bf16[8,192,512]{2,1,0:T(8,128)(2,1)S(1)} all-to-all(bf16[8,192,512]{2,1,0:T(8,128)(2,1)S(1)} %fusion.14), channel_id=1, replica_groups=mesh['group'=2,'dp'=8,'tensor'=8] {'dp'}, dimensions={0} | all-to-all | bytes 3145728 | tf_op jit(solution)/shard_map/all_to_all | solution.py:55
  409.6 21.1 %all_to_all.100 = bf16[8,192,512]{2,1,0:T(8,128)(2,1)} all-to-all(bf16[8,192,512]{2,1,0:T(8,128)(2,1)S(1)} %broadcast_in_dim.29), channel_id=1, replica_groups=mesh['group'=2,'dp'=8,'tensor'=8] {'dp'}, dimensions={0} | all-to-all | bytes 3145728 | tf_op jit(solution)/shard_map/all_to_all | solution.py:51
  439.7 10.6 %collective-permute-done.9 = bf16[192,1792]{1,0:T(8,128)(2,1)S(1)} collective-permute-done((bf16[192,1792]{1,0:T(8,128)(2,1)S(1)}, bf16[192,1792]{1,0:T(8,128)(2,1)S(1)}, u32[]{:S(2)}, u32[]{:S(2)}) %collective-permute-start.9) | collective-permute-done | bytes 688160 | tf_op jit(solution)/shard_map/ppermute | solution.py:29
  457.7 11.4 %fusion.15 = bf16[8,192,512]{2,1,0:T(8,128)(2,1)} fusion(bf16[8,512,1792]{2,1,0:T(8,128)(2,1)} %bitcast.142, bf16[192,1792]{1,0:T(8,128)(2,1)} %get-tuple-element.17), kind=kOutput, calls=%fused_computation.44 | convolution fusion | flops 2819358720 | bytes 16941056 | tf_op jit(solution)/shard_map/ru,bfu->brf/dot_general | solution.py:176
  475.8 14.7 %all-to-all-done.9 = bf16[8,192,512]{2,1,0:T(8,128)(2,1)S(1)} async-done(((bf16[8,192,512]{2,1,0:T(8,128)(2,1)}), bf16[8,192,512]{2,1,0:T(8,128)(2,1)S(1)}, u32[]{:S(2)}, u32[]{:S(2)}) %all-to-all-start.9) | async-done | bytes 1572896 | tf_op jit(solution)/shard_map/all_to_all | solution.py:55
  491.2 19.9 %all_to_all.101 = bf16[8,192,512]{2,1,0:T(8,128)(2,1)} all-to-all(bf16[8,192,512]{2,1,0:T(8,128)(2,1)S(1)} %broadcast_in_dim.32), channel_id=1, replica_groups=mesh['group'=2,'dp'=8,'tensor'=8] {'dp'}, dimensions={0} | all-to-all | bytes 3145728 | tf_op jit(solution)/shard_map/all_to_all | solution.py:51
  511.1 11.9 %fusion.48 = (bf16[192,1792]{1,0:T(8,128)(2,1)}, f32[192,1792]{1,0:T(8,128)}) fusion(bf16[8,192,512]{2,1,0:T(8,128)(2,1)} %all_to_all.101, bf16[8,1792,512]{2,1,0:T(8,128)(2,1)} %bitcast.147), kind=kOutput, calls=%fused_computation.106 | convolution fusion | flops 2818916352 | bytes 18317312 | tf_op jit(solution)/shard_map/brf,buf->ru/dot_general | solution.py:167
  523.3 14.5 %all-to-all-start.17 = ((bf16[8,192,512]{2,1,0:T(8,128)(2,1)}), bf16[8,192,512]{2,1,0:T(8,128)(2,1)}, u32[]{:S(2)}, u32[]{:S(2)}) async-start(bf16[8,192,512]{2,1,0:T(8,128)(2,1)} %all_to_all.100), calls=%async_computation.17 | async-start | bytes 3145728 | tf_op jit(solution)/shard_map/all_to_all | solution.py:64
  540.9 17.7 %all-to-all-done.17 = bf16[8,192,512]{2,1,0:T(8,128)(2,1)} async-done(((bf16[8,192,512]{2,1,0:T(8,128)(2,1)}), bf16[8,192,512]{2,1,0:T(8,128)(2,1)}, u32[]{:S(2)}, u32[]{:S(2)}) %all-to-all-start.17) | async-done | bytes 1572896 | tf_op jit(solution)/shard_map/all_to_all | solution.py:64
  562.8 11.8 %fusion.16 = bf16[8,192,512]{2,1,0:T(8,128)(2,1)} fusion(bf16[8,512,1792]{2,1,0:T(8,128)(2,1)} %bitcast.143, bf16[192,1792]{1,0:T(8,128)(2,1)} %get-tuple-element.7), kind=kOutput, calls=%fused_computation.45 | convolution fusion | flops 2819358720 | bytes 16941056 | tf_op jit(solution)/shard_map/ru,bfu->brf/dot_general | solution.py:176
  574.5 27.0 %all_to_all.102 = bf16[8,192,512]{2,1,0:T(8,128)(2,1)S(1)} all-to-all(bf16[8,192,512]{2,1,0:T(8,128)(2,1)} %fusion.16), channel_id=1, replica_groups=mesh['group'=2,'dp'=8,'tensor'=8] {'dp'}, dimensions={0} | all-to-all | bytes 3145728 | tf_op jit(solution)/shard_map/all_to_all | solution.py:55
  612.1 17.8 %all-to-all-done.18 = bf16[8,192,512]{2,1,0:T(8,128)(2,1)} async-done(((bf16[8,192,512]{2,1,0:T(8,128)(2,1)}), bf16[8,192,512]{2,1,0:T(8,128)(2,1)}, u32[]{:S(2)}, u32[]{:S(2)}) %all-to-all-start.18) | async-done | bytes 1572896 | tf_op jit(solution)/shard_map/all_to_all | solution.py:64
  631.1 14.4 %all-to-all-start.14 = ((bf16[8,192,512]{2,1,0:T(8,128)(2,1)}), bf16[8,192,512]{2,1,0:T(8,128)(2,1)S(1)}, u32[]{:S(2)}, u32[]{:S(2)}) async-start(bf16[8,192,512]{2,1,0:T(8,128)(2,1)} %broadcast_in_dim.35), calls=%async_computation.14 | async-start | bytes 3145728 | tf_op jit(solution)/shard_map/all_to_all | solution.py:51
  (172 shorter events, 237.2 us)
Async XLA Ops:
  7.2 130.1 %all-gather.10.cloned.1.call-start = ((), (), s32[]{:S(2)}) async-start(), calls=%async_computation.19 | async-start | bytes 6684672 | tf_op jit(solution)/shard_map/all_gather | solution.py:109
  9.1 212.9 %all-gather.12.cloned.1.call-start = ((), (), s32[]{:S(2)}) async-start(), calls=%async_computation.20 | async-start | bytes 1179648 | tf_op jit(solution)/shard_map/all_gather | solution.py:69
  10.6 215.5 %all-gather.14.cloned.1.call-start = ((), (), s32[]{:S(2)}) async-start(), calls=%async_computation.21 | async-start | bytes 16515072 | tf_op jit(solution)/shard_map/all_gather | solution.py:110
  11.3 275.2 %all-gather.24.cloned.1.call-start = ((), (), s32[]{:S(2)}) async-start(), calls=%async_computation.26 | async-start | bytes 16515072 | tf_op jit(solution)/shard_map/all_gather | solution.py:113
  13.2 32.1 %all-to-all-start = ((bf16[8,192,512]{2,1,0:T(8,128)(2,1)}), bf16[8,192,512]{2,1,0:T(8,128)(2,1)S(1)}, u32[]{:S(2)}, u32[]{:S(2)}) async-start(bf16[8,192,512]{2,1,0:T(8,128)(2,1)} %broadcast_in_dim.24), calls=%async_computation | async-start | bytes 3145728 | tf_op jit(solution)/shard_map/all_to_all | solution.py:51
  58.1 40.4 %all-to-all-start.1 = ((bf16[8,96,1024]{2,1,0:T(8,128)(2,1)}), bf16[8,96,1024]{2,1,0:T(8,128)(2,1)S(1)}, u32[]{:S(2)}, u32[]{:S(2)}) async-start(bf16[8,96,1024]{2,1,0:T(8,128)(2,1)} %fusion.6), calls=%async_computation.1 | async-start | bytes 3145728 | tf_op jit(solution)/shard_map/all_to_all | solution.py:55
  70.4 26.9 %collective-permute-start.1 = (bf16[3,512]{1,0:T(4,128)(2,1)S(1)}, bf16[3,512]{1,0:T(4,128)(2,1)S(1)}, u32[]{:S(2)}, u32[]{:S(2)}) collective-permute-start(bf16[3,512]{1,0:T(4,128)(2,1)S(1)} %slice.71), channel_id=1, source_target_pairs={{1,0},{2,1},{3,2},{4,3},{5,4},{6,5},{7,6},{9,8},{10,9},{11,10},{12... | collective-permute-start | bytes 9224 | tf_op jit(solution)/shard_map/ppermute | solution.py:46
  233.7 12.3 %collective-permute-start.6 = (bf16[192,1792]{1,0:T(8,128)(2,1)S(1)}, bf16[192,1792]{1,0:T(8,128)(2,1)S(1)}, u32[]{:S(2)}, u32[]{:S(2)}) collective-permute-start(bf16[192,1792]{1,0:T(8,128)(2,1)S(1)} %get-tuple-element.20), channel_id=1, source_target_pairs={{0,64},{64,0},{1,65},{65,1},{2,66},{66,2},{3,67},{67,3},{4,68},{68... | collective-permute-start | bytes 2064392 | tf_op jit(solution)/shard_map/ppermute | solution.py:29
  295.9 29.7 %all-to-all-start.5 = ((bf16[8,192,512]{2,1,0:T(8,128)(2,1)}), bf16[8,192,512]{2,1,0:T(8,128)(2,1)S(1)}, u32[]{:S(2)}, u32[]{:S(2)}) async-start(bf16[8,192,512]{2,1,0:T(8,128)(2,1)} %fusion.13), calls=%async_computation.5 | async-start | bytes 3145728 | tf_op jit(solution)/shard_map/all_to_all | solution.py:55
  302.6 354.8 %all-gather.20.cloned.1.call-start = ((), (), s32[]{:S(2)}) async-start(), calls=%async_computation.24 | async-start | bytes 6193152 | tf_op jit(solution)/shard_map/all_gather | solution.py:156
  363.4 13.5 %collective-permute-start.8 = (bf16[192,1792]{1,0:T(8,128)(2,1)S(1)}, bf16[192,1792]{1,0:T(8,128)(2,1)S(1)}, u32[]{:S(2)}, u32[]{:S(2)}) collective-permute-start(bf16[192,1792]{1,0:T(8,128)(2,1)S(1)} %get-tuple-element.22), channel_id=1, source_target_pairs={{0,64},{64,0},{1,65},{65,1},{2,66},{66,2},{3,67},{67,3},{4,68},{68... | collective-permute-start | bytes 2064392 | tf_op jit(solution)/shard_map/ppermute | solution.py:29
  378.1 295.7 %all-gather.22.cloned.1.call-start = ((), (), s32[]{:S(2)}) async-start(), calls=%async_computation.25 | async-start | bytes 6193152 | tf_op jit(solution)/shard_map/all_gather | solution.py:156
  378.7 328.0 %all-gather.16.cloned.1.call-start = ((), (), s32[]{:S(2)}) async-start(), calls=%async_computation.22 | async-start | bytes 6193152 | tf_op jit(solution)/shard_map/all_gather | solution.py:179
  453.8 15.3 %all-to-all-start.10 = ((f32[8,2,128]{2,1,0:T(2,128)}), f32[8,2,128]{2,1,0:T(2,128)S(1)}, u32[]{:S(2)}, u32[]{:S(2)}) async-start(f32[8,2,128]{2,1,0:T(2,128)} %broadcast_in_dim.31), calls=%async_computation.10 | async-start | bytes 16384 | tf_op jit(solution)/shard_map/all_to_all | solution.py:51
  469.2 21.4 %all-to-all-start.9 = ((bf16[8,192,512]{2,1,0:T(8,128)(2,1)}), bf16[8,192,512]{2,1,0:T(8,128)(2,1)S(1)}, u32[]{:S(2)}, u32[]{:S(2)}) async-start(bf16[8,192,512]{2,1,0:T(8,128)(2,1)} %fusion.15), calls=%async_computation.9 | async-start | bytes 3145728 | tf_op jit(solution)/shard_map/all_to_all | solution.py:55
  523.0 14.8 %collective-permute-start.10 = (bf16[192,1792]{1,0:T(8,128)(2,1)}, bf16[192,1792]{1,0:T(8,128)(2,1)}, u32[]{:S(2)}, u32[]{:S(2)}) collective-permute-start(bf16[192,1792]{1,0:T(8,128)(2,1)} %get-tuple-element.26), channel_id=1, source_target_pairs={{0,64},{64,0},{1,65},{65,1},{2,66},{66,2},{3,67},{67,3},{4,68},{68... | collective-permute-start | bytes 2064392 | tf_op jit(solution)/shard_map/ppermute | solution.py:29
  523.3 35.3 %all-to-all-start.17 = ((bf16[8,192,512]{2,1,0:T(8,128)(2,1)}), bf16[8,192,512]{2,1,0:T(8,128)(2,1)}, u32[]{:S(2)}, u32[]{:S(2)}) async-start(bf16[8,192,512]{2,1,0:T(8,128)(2,1)} %all_to_all.100), calls=%async_computation.17 | async-start | bytes 3145728 | tf_op jit(solution)/shard_map/all_to_all | solution.py:64
  537.8 181.9 %all-gather.18.cloned.1.call-start = ((), (), s32[]{:S(2)}) async-start(), calls=%async_computation.23 | async-start | bytes 6193152 | tf_op jit(solution)/shard_map/all_gather | solution.py:179
  559.2 15.3 %all-to-all-start.12 = ((f32[8,2,128]{2,1,0:T(2,128)}), f32[8,2,128]{2,1,0:T(2,128)S(1)}, u32[]{:S(2)}, u32[]{:S(2)}) async-start(f32[8,2,128]{2,1,0:T(2,128)} %broadcast_in_dim.34), calls=%async_computation.12 | async-start | bytes 16384 | tf_op jit(solution)/shard_map/all_to_all | solution.py:51
  601.5 28.3 %all-to-all-start.18 = ((bf16[8,192,512]{2,1,0:T(8,128)(2,1)}), bf16[8,192,512]{2,1,0:T(8,128)(2,1)}, u32[]{:S(2)}, u32[]{:S(2)}) async-start(bf16[8,192,512]{2,1,0:T(8,128)(2,1)} %all_to_all.101), calls=%async_computation.18 | async-start | bytes 3145728 | tf_op jit(solution)/shard_map/all_to_all | solution.py:64
  609.4 20.5 %collective-permute-start.15 = (bf16[192,512]{1,0:T(8,128)(2,1)S(1)}, bf16[192,512]{1,0:T(8,128)(2,1)S(1)}, u32[]{:S(2)}, u32[]{:S(2)}) collective-permute-start(bf16[192,512]{1,0:T(8,128)(2,1)S(1)} %fusion.31), channel_id=1, source_target_pairs={{0,0},{1,8},{2,16},{3,24},{4,32},{5,40},{6,48},{7,56},{8,1},{9,9},... | collective-permute-start | bytes 589832 | tf_op jit(solution)/shard_map/ppermute | solution.py:40
  631.1 37.3 %all-to-all-start.14 = ((bf16[8,192,512]{2,1,0:T(8,128)(2,1)}), bf16[8,192,512]{2,1,0:T(8,128)(2,1)S(1)}, u32[]{:S(2)}, u32[]{:S(2)}) async-start(bf16[8,192,512]{2,1,0:T(8,128)(2,1)} %broadcast_in_dim.35), calls=%async_computation.14 | async-start | bytes 3145728 | tf_op jit(solution)/shard_map/all_to_all | solution.py:51
  668.5 26.1 %all-to-all-start.15 = ((bf16[8,192,512]{2,1,0:T(8,128)(2,1)}), bf16[8,192,512]{2,1,0:T(8,128)(2,1)}, u32[]{:S(2)}, u32[]{:S(2)}) async-start(bf16[8,192,512]{2,1,0:T(8,128)(2,1)} %fusion.5), calls=%async_computation.15 | async-start | bytes 3145728 | tf_op jit(solution)/shard_map/all_to_all | solution.py:64
  694.6 25.1 %all-to-all-start.16 = ((bf16[8,192,512]{2,1,0:T(8,128)(2,1)}), bf16[8,192,512]{2,1,0:T(8,128)(2,1)S(1)}, u32[]{:S(2)}, u32[]{:S(2)}) async-start(bf16[8,192,512]{2,1,0:T(8,128)(2,1)} %fusion.2), calls=%async_computation.16 | async-start | bytes 3145728 | tf_op jit(solution)/shard_map/all_to_all | solution.py:64
  (29 other events, 332.2 us)
Sparse Core Ops, SparseCore 0:
  10.3 77.5 all-gather.9
  89.5 34.9 all-gather.11
  126.2 83.0 all-gather.13
  210.8 75.6 all-gather.23
  378.3 37.8 all-gather.19
  417.7 37.6 all-gather.21
  457.0 37.6 all-gather.15
  541.0 41.8 all-gather.17

commit v2 on v1

v2 whole, which is shorter than its diff:
```python
import functools
import math

import jax
import jax.numpy as jnp
from jax import lax
from jax.experimental import pallas as pl
from jax.experimental.pallas import tpu as pltpu
from jax.sharding import PartitionSpec as P

D = 8192
STEPS = 2
epsilon = 1e-05

F32 = jnp.float32
BF16 = jnp.bfloat16
UNITS = ("group", "tensor")
EVERY = ("group", "dp", "tensor")


def chip_peers():
    n = lax.axis_size(UNITS)
    return [[chip * 2 + core for chip in range(n // 2)] for core in range(2)]


def other_core(values):
    n = lax.axis_size("tensor")
    return lax.ppermute(values, "tensor", [(i, i ^ 1) for i in range(n)])


def other_group(values):
    return lax.ppermute(values, "group", [(0, 1), (1, 0)])


def swap_axes(values):
    groups, n = lax.axis_size("group"), lax.axis_size("dp")
    route = [
        ((k * n + a) * n + b, (k * n + b) * n + a)
        for k in range(groups)
        for a in range(n)
        for b in range(n)
    ]
    return lax.ppermute(values, EVERY, route)


def shifted(block, axis, distance):
    devices = range(lax.axis_size(axis))
    route = [(i - distance, i) for i in devices if i - distance in devices]
    return lax.ppermute(block, axis, route)


def copies(values, axis, count, groups=None):
    sent = jnp.broadcast_to(values[None], (count,) + values.shape)
    return lax.all_to_all(sent, axis, 0, 0, tiled=True, axis_index_groups=groups)


def total_of(blocks, axis, groups=None):
    got = lax.all_to_all(blocks, axis, 0, 0, tiled=True, axis_index_groups=groups)
    return jnp.sum(got.astype(F32), axis=0)


def contract_rows(left, right):
    return lax.dot_general(left, right, (((0,), (0,)), ((), ())), preferred_element_type=F32)


def to_feature_owners(blocks):
    return lax.all_to_all(blocks, "tensor", 0, 0, tiled=True)


def chip_order(own, other, core):
    pair = jnp.where(core == 0, jnp.stack([own, other], axis=1), jnp.stack([other, own], axis=1))
    return pair.reshape((own.shape[0] * 2,) + own.shape[1:])


def blocks_in_kernel(flipped, left, weight, out, total):
    step = pl.program_id(0)
    dims = (((1,), (1 if flipped else 0,)), ((), ()))
    part = lax.dot_general(left[0], weight[0], dims, preferred_element_type=F32)
    for k in range(1, left.shape[0]):
        part += lax.dot_general(left[k], weight[k], dims, preferred_element_type=F32)

    @pl.when(step == 0)
    def _():
        total[...] = part

    @pl.when(step > 0)
    def _():
        total[...] += part

    @pl.when(step == pl.num_programs(0) - 1)
    def _():
        out[...] = total[...].astype(out.dtype)


def product_in(left, weight, flipped, half, halves, each=2):
    n, rows, width = left.shape
    units = weight.shape[1 if flipped else 2] // halves
    if flipped:
        spec = pl.BlockSpec((each, units, width), lambda b: (b, half, 0))
    else:
        spec = pl.BlockSpec((each, width, units), lambda b: (b, 0, half))
    return pl.pallas_call(
        functools.partial(blocks_in_kernel, flipped),
        grid=(n // each,),
        in_specs=[pl.BlockSpec((each, rows, width), lambda b: (b, 0, 0)), spec],
        out_specs=pl.BlockSpec((rows, units), lambda b: (0, 0)),
        out_shape=jax.ShapeDtypeStruct((rows, units), BF16),
        scratch_shapes=[pltpu.VMEM((rows, units), F32)],
        compiler_params=pltpu.CompilerParams(vmem_limit_bytes=40 << 20),
        cost_estimate=pl.CostEstimate(
            flops=2 * n * rows * width * units,
            bytes_accessed=2 * n * width * (rows + units),
            transcendentals=0,
        ),
        name="product_in",
    )(left, weight)


def blocks_out_kernel(flipped, left, weight, *rest):
    out = rest[-1]
    rows = left.shape[0]
    dims = (((1,), (1 if flipped else 0,)), ((), ()))
    for k in range(weight.shape[0]):
        product = lax.dot_general(left[...], weight[k], dims, preferred_element_type=F32)
        out[k, :rows] = product.astype(out.dtype)
        if len(rest) == 2:
            out[k, rows:] = rest[0][...]


def product_out(left, weight, flipped, added=None, each=2):
    rows, units = left.shape
    n, first, second = weight.shape
    width = first if flipped else second
    extra = [] if added is None else [added]
    height = rows + sum(e.shape[0] for e in extra)
    return pl.pallas_call(
        functools.partial(blocks_out_kernel, flipped),
        grid=(n // each,),
        in_specs=[
            pl.BlockSpec((rows, units), lambda b: (0, 0)),
            pl.BlockSpec((each, first, second), lambda b: (b, 0, 0)),
        ]
        + [pl.BlockSpec(e.shape, lambda b: (0, 0)) for e in extra],
        out_specs=pl.BlockSpec((each, height, width), lambda b: (b, 0, 0)),
        out_shape=jax.ShapeDtypeStruct((n, height, width), BF16),
        compiler_params=pltpu.CompilerParams(vmem_limit_bytes=40 << 20),
        cost_estimate=pl.CostEstimate(
            flops=2 * n * rows * width * units,
            bytes_accessed=2 * n * width * (rows + units),
            transcendentals=0,
        ),
        name="product_out",
    )(left, weight, *extra)


def in_pieces(values, count, width):
    rows, rest = [], values
    for _ in range(3):
        rows.append(rest.astype(BF16))
        rest = rest - rows[-1].astype(F32)
    return jnp.pad(jnp.stack(rows), ((0, count - 3), (0, width - values.shape[0])))


def summed_in(left, weight, flipped, halves=2):
    own = [product_in(left, weight, flipped, k, halves) for k in range(halves)]
    other = [other_group(part) for part in own]
    return [p.astype(F32) + o.astype(F32) for p, o in zip(own, other)]


def after(values, *earlier):
    for other in earlier:
        first = other[(0,) * other.ndim].astype(F32)
        values = values + (0.0 * first).astype(values.dtype)
    return values


def body(
    context,
    low,
    mid,
    top,
    segments,
    output_weight,
    join_weight,
    inner_weight,
    outer_weight,
    norm_gain,
):
    n_dp = lax.axis_size("dp")
    n_tensor = lax.axis_size("tensor")
    chips = lax.axis_size(UNITS) // 2
    rows, width = context.shape
    rows_b, width_b = low.shape
    tokens = rows * n_dp
    core = lax.axis_index("tensor") % 2
    peers = chip_peers()
    place = lax.axis_index("tensor") * rows

    own_top = swap_axes(top)
    gain = norm_gain[:, None]
    following_top = shifted(own_top[: STEPS + 1], "tensor", -1)
    top_ext = jnp.concatenate([own_top, following_top], axis=0).astype(F32)
    seg_pad = jnp.concatenate([segments, jnp.full((STEPS + 1,), -1, jnp.int32)])
    seg_window = lax.dynamic_slice_in_dim(seg_pad, place, rows + STEPS + 1, 0)

    first_group = lax.axis_index("group") == 0
    hidden_all = []
    near = lax.all_gather(jnp.concatenate([low, mid], axis=1), "tensor", axis=0, tiled=True)
    half = near.reshape(n_tensor // 2, 2, rows_b, 2 * width_b)
    far_own = other_group(lax.dynamic_index_in_dim(half, core, 1, keepdims=False))
    far = chip_order(far_own, other_core(far_own), core).reshape(near.shape)
    for k in range(2):
        ours, theirs = (v[:, k * width_b : (k + 1) * width_b] for v in (near, far))
        hidden_all.append(
            jnp.where(
                first_group,
                jnp.concatenate([ours, theirs], axis=0),
                jnp.concatenate([theirs, ours], axis=0),
            )
        )
    gained = (inner_weight.astype(F32) * gain).astype(BF16)
    inner_all = lax.all_gather(gained, "tensor", axis=0, tiled=True)
    inner_all = inner_all.reshape(n_tensor, width, -1)
    outer_all = lax.all_gather(outer_weight, "tensor", axis=0, tiled=False)

    context_all = copies(context, "dp", n_dp).reshape(tokens, width)
    part = jnp.dot(context_all, output_weight, preferred_element_type=F32)
    part = after(part, own_top).astype(BF16)
    part = part.reshape(chips, 2, rows_b, width_b)
    kept = lax.dynamic_index_in_dim(part, core, 1, keepdims=False)
    given = lax.dynamic_index_in_dim(part, 1 - core, 1, keepdims=False)
    part = (kept.astype(F32) + other_core(given).astype(F32)).astype(BF16)
    high = after(mid.astype(F32), far_own, following_top) + total_of(part, UNITS, peers)
    high = high.astype(BF16)
    high_own = copies(high, UNITS, chips, peers)
    high_other = other_core(high_own)
    high_all = chip_order(high_own, high_other, core).reshape(tokens, width_b)
    hidden_all.append(high_all)

    joined = jnp.dot(hidden_all[0], join_weight[0], preferred_element_type=F32)
    joined = joined + jnp.dot(hidden_all[1], join_weight[1], preferred_element_type=F32)
    joined = joined + jnp.dot(hidden_all[2], join_weight[2], preferred_element_type=F32)
    joined = total_of(joined.astype(BF16).reshape(n_dp, rows, width), "dp")
    joined = joined.astype(BF16)
    state = swap_axes(joined)
    x_tokens = [lax.all_gather(joined, "dp", axis=0, tiled=True)]

    saved = []
    total = jnp.zeros((), F32)
    for step in range(STEPS):
        xfull = state.astype(F32)
        x_all = copies(state, "dp", n_dp)
        if step > 0:
            x_tokens.append(to_feature_owners(x_all).reshape(tokens, width))
        x_wide = x_all.astype(F32)
        sums = jnp.sum(x_wide * x_wide, axis=(0, 2))
        sums = sums + other_group(sums)
        scale = lax.rsqrt(sums / D + epsilon)[:, None]
        inner = scale * jnp.concatenate(summed_in(x_all, inner_all, False), axis=1)
        if step > 0:
            inner = after(inner, saved[0][3])
        active = jax.nn.silu(inner).astype(BF16)
        update = total_of(product_out(active, outer_all, False), "dp")
        following = (xfull + update).astype(BF16)
        valid = (seg_window[step + 1 : step + 1 + rows] == seg_window[:rows]).astype(F32)
        error = valid[:, None] * (following.astype(F32) - top_ext[step + 1 : step + 1 + rows])
        total = total + jnp.sum(error * error)
        active_all = lax.all_gather(active, "tensor", axis=0, tiled=True)
        saved.append((xfull, scale, inner, active_all, error))
        state = following
    scaled_all, sources = [], []
    rate = 1.0 / math.sqrt(tokens)
    grad = jnp.zeros((rows, width), F32)
    grad_inner = jnp.zeros(inner_weight.shape, F32)
    grad_outer = jnp.zeros(outer_weight.shape, F32)
    for step in reversed(range(STEPS)):
        xfull, scale, inner, active_all, error = saved[step]
        grad = grad + rate * error
        grad_half = grad.astype(BF16)
        grad_all = copies(grad_half, "dp", n_dp)
        grad_tokens = to_feature_owners(grad_all)
        back_act = jnp.concatenate(summed_in(grad_all, outer_all, True), axis=1)
        if step == 0:
            back_act = after(back_act, grad_tokens)
        if step < STEPS - 1:
            back_act = after(back_act, mean_error)
        else:
            back_act = after(back_act, *x_tokens)
        grad_tokens = grad_tokens.reshape(tokens, width)
        sigma = jax.nn.sigmoid(inner)
        grad_in = (back_act * sigma * (1.0 + inner * (1.0 - sigma))).astype(BF16)
        grad_in_wide = grad_in.astype(F32)
        moved = jnp.sum(grad_in_wide * inner, axis=1)
        moved = in_pieces(jnp.concatenate([moved, total[None]]), 16, width)
        back = total_of(product_out(grad_in, inner_all, True, moved), "dp")
        back_norm = back[:rows]
        moved = back[rows] + back[rows + 1] + back[rows + 2]
        if step == STEPS - 1:
            total_dp = jnp.broadcast_to(moved[rows], (128,))
        moved = moved[:rows, None]
        grad = grad + scale * back_norm - xfull * scale**2 * moved / D
        sources.append((active_all, grad_tokens))
        if step == 0:
            grad_outer = contract_rows(active_all, grad_tokens)
            grad = after(grad, grad_outer)
        scaled = (scale * grad_in_wide).astype(BF16)
        scaled_all.append(lax.all_gather(scaled, "tensor", axis=0, tiled=True))
        if step == STEPS - 1:
            for k in (1, 2, 4):
                total_dp = total_dp + lax.ppermute(
                    total_dp, "tensor", [(i, i ^ k) for i in range(n_tensor)]
                )
            mean_error = (total_dp + other_group(total_dp))[0] / (STEPS * tokens * D)
    swapped = after(swap_axes(grad.astype(BF16)), *[source[1] for source in sources])
    for units, features in sources[:-1]:
        grad_outer = grad_outer + contract_rows(units, features)
    for step, units in zip(reversed(range(STEPS)), scaled_all):
        grad_inner = grad_inner + gain * contract_rows(x_tokens[step], units)
    grad_tokens = copies(swapped, "dp", n_dp).reshape(tokens, width)
    grad_tokens = after(grad_tokens, grad_inner, grad_outer)
    grad_join = jnp.stack([contract_rows(source, grad_tokens) for source in hidden_all])
    return (mean_error, grad_join, grad_inner, grad_outer)


def solution(mesh):
    in_specs = (
        P("dp", ("group", "tensor")),
        P(("group", "tensor"), "dp"),
        P(("group", "tensor"), "dp"),
        P("dp", ("group", "tensor")),
        P(),
        P(("group", "tensor"), "dp"),
        P(None, "dp", ("group", "tensor")),
        P(("group", "tensor"), "dp"),
        P("dp", ("group", "tensor")),
        P(("group", "tensor")),
    )
    out_specs = (
        P(),
        P(None, "dp", ("group", "tensor")),
        P(("group", "tensor"), "dp"),
        P("dp", ("group", "tensor")),
    )
    return jax.shard_map(body, mesh=mesh, in_specs=in_specs, out_specs=out_specs, check_vma=False)
```

time: 748 us -> 699 us (0.934)
  matrix products: 134 us -> 39.8 us
  Pallas kernels: 0 us -> 77.1 us
  waiting for transfers between devices: 238 us -> 195 us
  local copies, waits for them, and re-layouts: 10.6 us -> 35.5 us
  blocking collectives: 210 us -> 187 us
  other arithmetic: 26.5 us -> 34.4 us
    pallas_call x0 -> x12, Pallas kernels: none -> 77.1 us  [the longest x8 44.8 us: product_in(): pl.pallas_call(functools.partial(blocks_in_kernel, flipped), grid=(n // e...]
    dot_general x9 -> x1, matrix products: 78.3 us -> 1.8 us  [body(): part = jnp.dot(context_all, output_weight, preferred_element_type=F32)]
    all_to_all x5 -> x3, blocking collectives: 132 us -> 85.8 us  [copies(): lax.all_to_all(sent, axis, 0, 0, tiled=True, axis_index_groups=groups)]
    all_gather x1, waiting for transfers between devices: 40 us -> 0.02 us  [body(): outer_all = lax.all_gather(outer_weight, 'tensor', axis=0, tiled=False)]
    all_to_all x4, waiting for transfers between devices: 26.9 us -> 53.3 us  [copies(): lax.all_to_all(sent, axis, 0, 0, tiled=True, axis_index_groups=groups)]
    all_to_all x4 -> x3, waiting for transfers between devices: 42.2 us -> 16.6 us  [to_feature_owners(): return lax.all_to_all(blocks, 'tensor', 0, 0, tiled=True)]
    all_to_all x3 -> x4, blocking collectives: 77.2 us -> 101 us  [total_of(): lax.all_to_all(blocks, axis, 0, 0, tiled=True, axis_index_groups=groups)]
    ppermute x3, waiting for transfers between devices: 9.21 us -> 29.8 us  [swap_axes(): return lax.ppermute(values, EVERY, route)]
  transfers between devices with their start and end apart: 35 -> 39, of which waited for: 23 -> 18; matrix products, arithmetic and copies ran while one was open for 19% -> 13% of each run, Pallas kernels for 0% -> 11%
where the time goes in v2:
time: 699 us; the launch traced here: 692 us
  waiting for transfers between devices  195 us (28%)
  blocking collectives  187 us (27%)
  starting transfers between devices  98.1 us (14%)
  Pallas kernels  77.1 us (11%)
  matrix products  39.8 us (6%)
  local copies, waits for them, and re-layouts  35.5 us (5%)
  other arithmetic  34.4 us (5%)
  between operations  25.6 us (4%)
    all_to_all x4, blocking collectives, total_of(): lax.all_to_all(blocks, axis, 0, 0, tiled=True, axis_index_groups=groups)  101 us
    all_to_all x3, blocking collectives, copies(): lax.all_to_all(sent, axis, 0, 0, tiled=True, axis_index_groups=groups)  85.8 us
    all_to_all x4, waiting for transfers between devices, copies(): lax.all_to_all(sent, axis, 0, 0, tiled=True, axis_index_groups=groups)  53.3 us
    pallas_call x8, Pallas kernels, product_in(): pl.pallas_call(functools.partial(blocks_in_kernel, flipped), grid=(n // e...  44.8 us
    ppermute x1, waiting for transfers between devices, shifted(): return lax.ppermute(block, axis, route)  34.8 us
    dot_general x7, matrix products, contract_rows(): lax.dot_general(left, right, (((0,), (0,)), ((), ())), preferred_element_...  32.5 us
    pallas_call x4, Pallas kernels, product_out(): pl.pallas_call(functools.partial(blocks_out_kernel, flipped), grid=(n //...  32.3 us
    ppermute x3, waiting for transfers between devices, swap_axes(): return lax.ppermute(values, EVERY, route)  29.8 us
  transfers between devices with their start and end apart: 39, of which 18 were waited for; matrix products, arithmetic and copies ran while one was open for 13% of the time, Pallas kernels for 11%

profile of v2, /device:TPU:1, one launch (start us, length us, event | category | flops | bytes accessed | tf_op | source)
XLA Modules:
  0.0 692.4 jit_solution(3403032977967346424)
XLA Ops:
  14.5 8.5 %all-to-all-start = ((bf16[8,192,512]{2,1,0:T(8,128)(2,1)}), bf16[8,192,512]{2,1,0:T(8,128)(2,1)S(1)}, u32[]{:S(2)}, u32[]{:S(2)}) async-start(bf16[8,192,512]{2,1,0:T(8,128)(2,1)} %broadcast_in_dim.16), calls=%async_computation | async-start | bytes 3145728 | tf_op jit(solution)/shard_map/all_to_all | solution.py:54
  27.4 25.6 %collective-permute-done.2 = bf16[192,512]{1,0:T(8,128)(2,1)S(1)} collective-permute-done((bf16[192,512]{1,0:T(8,128)(2,1)S(1)}, bf16[192,512]{1,0:T(8,128)(2,1)S(1)}, u32[]{:S(2)}, u32[]{:S(2)}) %collective-permute-start.2) | collective-permute-done | bytes 196640 | tf_op jit(solution)/shard_map/ppermute | solution.py:43
  71.2 34.8 %collective-permute-done.3 = bf16[3,512]{1,0:T(4,128)(2,1)S(1)} collective-permute-done((bf16[3,512]{1,0:T(4,128)(2,1)S(1)}, bf16[3,512]{1,0:T(4,128)(2,1)S(1)}, u32[]{:S(2)}, u32[]{:S(2)}) %collective-permute-start.3) | collective-permute-done | bytes 3104 | tf_op jit(solution)/shard_map/ppermute | solution.py:49
  124.8 30.9 %all-to-all-done.2 = bf16[8,96,1024]{2,1,0:T(8,128)(2,1)} async-done(((bf16[8,96,1024]{2,1,0:T(8,128)(2,1)}), bf16[8,96,1024]{2,1,0:T(8,128)(2,1)}, u32[]{:S(2)}, u32[]{:S(2)}) %all-to-all-start.2) | async-done | bytes 1572896 | tf_op jit(solution)/shard_map/all_to_all | solution.py:54
  171.5 29.3 %all_to_all.80 = bf16[8,192,512]{2,1,0:T(8,128)(2,1)S(1)} all-to-all(bf16[8,192,512]{2,1,0:T(8,128)(2,1)S(1)} %bitcast.100), channel_id=1, replica_groups=mesh['group'=2,'dp'=8,'tensor'=8] {'dp'}, dimensions={0} | all-to-all | bytes 3145728 | tf_op jit(solution)/shard_map/all_to_all | solution.py:58
  208.5 39.9 %all_to_all.81.left = bf16[8,192,512]{2,1,0:T(8,128)(2,1)S(1)} all-to-all(bf16[8,192,512]{2,1,0:T(8,128)(2,1)S(1)} %broadcast_in_dim.18), channel_id=1, replica_groups=mesh['group'=2,'dp'=8,'tensor'=8] {'dp'}, dimensions={0} | all-to-all | bytes 3145728 | tf_op jit(solution)/shard_map/all_to_all | solution.py:54
  261.9 8.3 %collective-permute-done.8 = bf16[192,896]{1,0:T(8,128)(2,1)S(1)} collective-permute-done((bf16[192,896]{1,0:T(8,128)(2,1)S(1)}, bf16[192,896]{1,0:T(8,128)(2,1)S(1)}, u32[]{:S(2)}, u32[]{:S(2)}) %collective-permute-start.8) | collective-permute-done | bytes 344096 | tf_op jit(solution)/shard_map/ppermute | solution.py:32
  272.7 8.1 %product_out.4 = bf16[8,192,512]{2,1,0:T(8,128)(2,1)} custom-call(bf16[192,1792]{1,0:T(8,128)(2,1)S(1)} %copy-done.3, bf16[8,1792,512]{2,1,0:T(8,128)(2,1)} %bitcast.82), custom_call_target="tpu_custom_call" | custom-call | flops 2818572288 | bytes 16252928 | tf_op jit(solution)/shard_map/product_out/pallas_call | solution.py:136
  285.5 22.7 %all-to-all-done.5 = bf16[8,192,512]{2,1,0:T(8,128)(2,1)} async-done(((bf16[8,192,512]{2,1,0:T(8,128)(2,1)}), bf16[8,192,512]{2,1,0:T(8,128)(2,1)}, u32[]{:S(2)}, u32[]{:S(2)}) %all-to-all-start.5) | async-done | bytes 1572896 | tf_op jit(solution)/shard_map/all_to_all | solution.py:58
  316.9 22.3 %all-to-all-done.6.left = bf16[8,192,512]{2,1,0:T(8,128)(2,1)} async-done(((bf16[8,192,512]{2,1,0:T(8,128)(2,1)}), bf16[8,192,512]{2,1,0:T(8,128)(2,1)}, u32[]{:S(2)}, u32[]{:S(2)}) %all-to-all-start.6) | async-done | bytes 1572896 | tf_op jit(solution)/shard_map/all_to_all | solution.py:54
  357.7 14.8 %collective-permute-done.11 = bf16[192,896]{1,0:T(8,128)(2,1)S(1)} collective-permute-done((bf16[192,896]{1,0:T(8,128)(2,1)S(1)}, bf16[192,896]{1,0:T(8,128)(2,1)S(1)}, u32[]{:S(2)}, u32[]{:S(2)}) %collective-permute-start.11) | collective-permute-done | bytes 344096 | tf_op jit(solution)/shard_map/ppermute | solution.py:32
  384.1 22.6 %all_to_all.82 = bf16[8,192,512]{2,1,0:T(8,128)(2,1)S(1)} all-to-all(bf16[8,192,512]{2,1,0:T(8,128)(2,1)S(1)} %product_out.5), channel_id=1, replica_groups=mesh['group'=2,'dp'=8,'tensor'=8] {'dp'}, dimensions={0} | all-to-all | bytes 3145728 | tf_op jit(solution)/shard_map/all_to_all | solution.py:58
  408.6 22.3 %all_to_all.83.left = bf16[8,192,512]{2,1,0:T(8,128)(2,1)} all-to-all(bf16[8,192,512]{2,1,0:T(8,128)(2,1)S(1)} %broadcast_in_dim.20), channel_id=1, replica_groups=mesh['group'=2,'dp'=8,'tensor'=8] {'dp'}, dimensions={0} | all-to-all | bytes 3145728 | tf_op jit(solution)/shard_map/all_to_all | solution.py:54
  430.9 12.3 %all-to-all-start.9 = ((bf16[8,192,512]{2,1,0:T(8,128)(2,1)}), bf16[8,192,512]{2,1,0:T(8,128)(2,1)}, u32[]{:S(2)}, u32[]{:S(2)}) async-start(bf16[8,192,512]{2,1,0:T(8,128)(2,1)} %all-to-all-done.6.left), calls=%async_computation.9 | async-start | bytes 3145728 | tf_op jit(solution)/shard_map/all_to_all | solution.py:67
  471.4 8.6 %product_out.6 = bf16[8,208,512]{2,1,0:T(8,128)(2,1)S(1)} custom-call(bf16[192,1792]{1,0:T(8,128)(2,1)S(1)} %get-tuple-element.7.left, bf16[8,512,1792]{2,1,0:T(8,128)(2,1)} %bitcast.80, bf16[16,512]{1,0:T(8,128)(2,1)S(1)} %fusion.46.rest_0_), custom_call_target="tpu_custom_call" | custom-call | flops 2818572288 | bytes 16252928 | tf_op jit(solution)/shard_map/product_out/pallas_call | solution.py:136
  480.0 25.2 %all_to_all.84 = bf16[8,208,512]{2,1,0:T(8,128)(2,1)S(1)} all-to-all(bf16[8,208,512]{2,1,0:T(8,128)(2,1)S(1)} %product_out.6), channel_id=1, replica_groups=mesh['group'=2,'dp'=8,'tensor'=8] {'dp'}, dimensions={0} | all-to-all | bytes 3407872 | tf_op jit(solution)/shard_map/all_to_all | solution.py:58
  507.5 23.6 %all_to_all.85.left = bf16[8,192,512]{2,1,0:T(8,128)(2,1)} all-to-all(bf16[8,192,512]{2,1,0:T(8,128)(2,1)S(1)} %broadcast_in_dim.22), channel_id=1, replica_groups=mesh['group'=2,'dp'=8,'tensor'=8] {'dp'}, dimensions={0} | all-to-all | bytes 3145728 | tf_op jit(solution)/shard_map/all_to_all | solution.py:54
  531.1 7.7 %all-to-all-start.12 = ((bf16[8,192,512]{2,1,0:T(8,128)(2,1)}), bf16[8,192,512]{2,1,0:T(8,128)(2,1)}, u32[]{:S(2)}, u32[]{:S(2)}) async-start(bf16[8,192,512]{2,1,0:T(8,128)(2,1)} %all_to_all.85.left), calls=%async_computation.12 | async-start | bytes 3145728 | tf_op jit(solution)/shard_map/all_to_all | solution.py:67
  569.7 8.3 %product_out.7 = bf16[8,208,512]{2,1,0:T(8,128)(2,1)S(1)} custom-call(bf16[192,1792]{1,0:T(8,128)(2,1)S(1)} %get-tuple-element.5.left, bf16[8,512,1792]{2,1,0:T(8,128)(2,1)} %bitcast.81, bf16[16,512]{1,0:T(8,128)(2,1)S(1)} %fusion.51.rest_0_), custom_call_target="tpu_custom_call" | custom-call | flops 2818572288 | bytes 16252928 | tf_op jit(solution)/shard_map/product_out/pallas_call | solution.py:136
  578.1 24.0 %all_to_all.86 = bf16[8,208,512]{2,1,0:T(8,128)(2,1)S(1)} all-to-all(bf16[8,208,512]{2,1,0:T(8,128)(2,1)S(1)} %product_out.7), channel_id=1, replica_groups=mesh['group'=2,'dp'=8,'tensor'=8] {'dp'}, dimensions={0} | all-to-all | bytes 3407872 | tf_op jit(solution)/shard_map/all_to_all | solution.py:58
  602.1 7.9 %all-to-all-start.14 = ((bf16[8,192,512]{2,1,0:T(8,128)(2,1)}), bf16[8,192,512]{2,1,0:T(8,128)(2,1)S(1)}, u32[]{:S(2)}, u32[]{:S(2)}) async-start(bf16[8,192,512]{2,1,0:T(8,128)(2,1)} %all_to_all.83.left), calls=%async_computation.14 | async-start | bytes 3145728 | tf_op jit(solution)/shard_map/all_to_all | solution.py:67
  619.9 10.9 %all-to-all-done.14 = bf16[8,192,512]{2,1,0:T(8,128)(2,1)S(1)} async-done(((bf16[8,192,512]{2,1,0:T(8,128)(2,1)}), bf16[8,192,512]{2,1,0:T(8,128)(2,1)S(1)}, u32[]{:S(2)}, u32[]{:S(2)}) %all-to-all-start.14) | async-done | bytes 1572896 | tf_op jit(solution)/shard_map/all_to_all | solution.py:67
  635.2 11.4 %all-to-all-start.15 = ((bf16[8,192,512]{2,1,0:T(8,128)(2,1)}), bf16[8,192,512]{2,1,0:T(8,128)(2,1)S(1)}, u32[]{:S(2)}, u32[]{:S(2)}) async-start(bf16[8,192,512]{2,1,0:T(8,128)(2,1)} %broadcast_in_dim.23), calls=%async_computation.15 | async-start | bytes 3145728 | tf_op jit(solution)/shard_map/all_to_all | solution.py:54
  655.9 8.0 %fusion.74 = f32[512,1792]{1,0:T(8,128)} fusion(bf16[1536,512]{1,0:T(8,128)(2,1)} %bitcast.23, bf16[1536,1792]{1,0:T(8,128)(2,1)} %all-gather.18.cloned.1.call-done), kind=kOutput, calls=%fused_computation.147 | convolution fusion | flops 2818572288 | bytes 10747904 | tf_op jit(solution)/shard_map/dot_general | solution.py:63
  (248 shorter events, 228.5 us)
Async XLA Ops:
  7.2 51.1 %all-gather.10.cloned.1.call-start = ((), (), s32[]{:S(2)}) async-start(), calls=%async_computation.16 | async-start | bytes 3538944 | tf_op jit(solution)/shard_map/all_gather | solution.py:208
  9.1 240.4 %all-gather.12.cloned.1.call-start = ((), (), s32[]{:S(2)}) async-start(), calls=%async_computation.17 | async-start | bytes 16515072 | tf_op jit(solution)/shard_map/all_gather | solution.py:222
  12.3 259.3 %all-gather.24.cloned.1.call-start = ((), (), s32[]{:S(2)}) async-start(), calls=%async_computation.23 | async-start | bytes 16515072 | tf_op jit(solution)/shard_map/all_gather | solution.py:224
  14.5 39.7 %all-to-all-start = ((bf16[8,192,512]{2,1,0:T(8,128)(2,1)}), bf16[8,192,512]{2,1,0:T(8,128)(2,1)S(1)}, u32[]{:S(2)}, u32[]{:S(2)}) async-start(bf16[8,192,512]{2,1,0:T(8,128)(2,1)} %broadcast_in_dim.16), calls=%async_computation | async-start | bytes 3145728 | tf_op jit(solution)/shard_map/all_to_all | solution.py:54
  22.9 30.1 %collective-permute-start.2 = (bf16[192,512]{1,0:T(8,128)(2,1)S(1)}, bf16[192,512]{1,0:T(8,128)(2,1)S(1)}, u32[]{:S(2)}, u32[]{:S(2)}) collective-permute-start(bf16[192,512]{1,0:T(8,128)(2,1)S(1)} %copy-done.34), channel_id=1, source_target_pairs={{0,0},{1,8},{2,16},{3,24},{4,32},{5,40},{6,48},{7,56},{8,1},{9,9},... | collective-permute-start | bytes 589832 | tf_op jit(solution)/shard_map/ppermute | solution.py:43
  59.9 52.8 %collective-permute-start = (bf16[4,96,2048]{2,1,0:T(8,128)(2,1)S(1)}, bf16[4,96,2048]{2,1,0:T(8,128)(2,1)}, u32[]{:S(2)}, u32[]{:S(2)}) collective-permute-start(bf16[4,96,2048]{2,1,0:T(8,128)(2,1)S(1)} %dynamic-slice_bitcast_fusion.1), channel_id=1, source_target_pairs={{0,64},{64,0},{1,65},{65,1},{2,66},{66,2},{3,67},{67,3},{4,68},{68... | collective-permute-start | bytes 4718600 | tf_op jit(solution)/shard_map/ppermute | solution.py:32
  63.7 48.7 %all-to-all-start.1 = ((bf16[8,96,1024]{2,1,0:T(8,128)(2,1)}), bf16[8,96,1024]{2,1,0:T(8,128)(2,1)S(1)}, u32[]{:S(2)}, u32[]{:S(2)}) async-start(bf16[8,96,1024]{2,1,0:T(8,128)(2,1)} %fusion), calls=%async_computation.1 | async-start | bytes 3145728 | tf_op jit(solution)/shard_map/all_to_all | solution.py:58
  68.5 37.5 %collective-permute-start.3 = (bf16[3,512]{1,0:T(4,128)(2,1)S(1)}, bf16[3,512]{1,0:T(4,128)(2,1)S(1)}, u32[]{:S(2)}, u32[]{:S(2)}) collective-permute-start(bf16[3,512]{1,0:T(4,128)(2,1)S(1)} %slice.163), channel_id=1, source_target_pairs={{1,0},{2,1},{3,2},{4,3},{5,4},{6,5},{7,6},{9,8},{10,9},{11,10},{12... | collective-permute-start | bytes 9224 | tf_op jit(solution)/shard_map/ppermute | solution.py:49
  114.5 42.0 %collective-permute-start.1 = (bf16[4,96,2048]{2,1,0:T(8,128)(2,1)}, bf16[4,96,2048]{2,1,0:T(8,128)(2,1)}, u32[]{:S(2)}, u32[]{:S(2)}) collective-permute-start(bf16[4,96,2048]{2,1,0:T(8,128)(2,1)} %collective-permute-done), channel_id=1, source_target_pairs={{0,1},{1,0},{2,3},{3,2},{4,5},{5,4},{6,7},{7,6},{8,9},{9,8},{10,11... | collective-permute-start | bytes 4718600 | tf_op jit(solution)/shard_map/ppermute | solution.py:28
  117.3 38.4 %all-to-all-start.2 = ((bf16[8,96,1024]{2,1,0:T(8,128)(2,1)}), bf16[8,96,1024]{2,1,0:T(8,128)(2,1)}, u32[]{:S(2)}, u32[]{:S(2)}) async-start(bf16[8,96,1024]{2,1,0:T(8,128)(2,1)} %broadcast_in_dim.17), calls=%async_computation.2 | async-start | bytes 3145728 | tf_op jit(solution)/shard_map/all_to_all | solution.py:54
  122.7 249.9 %all-gather.14.cloned.1.call-start = ((), (), s32[]{:S(2)}) async-start(), calls=%async_computation.18 | async-start | bytes 6193152 | tf_op jit(solution)/shard_map/all_gather | solution.py:268
  280.8 27.4 %all-to-all-start.5 = ((bf16[8,192,512]{2,1,0:T(8,128)(2,1)}), bf16[8,192,512]{2,1,0:T(8,128)(2,1)}, u32[]{:S(2)}, u32[]{:S(2)}) async-start(bf16[8,192,512]{2,1,0:T(8,128)(2,1)} %product_out.4), calls=%async_computation.5 | async-start | bytes 3145728 | tf_op jit(solution)/shard_map/all_to_all | solution.py:58
  312.0 27.3 %all-to-all-start.6 = ((bf16[8,192,512]{2,1,0:T(8,128)(2,1)}), bf16[8,192,512]{2,1,0:T(8,128)(2,1)}, u32[]{:S(2)}, u32[]{:S(2)}) async-start(bf16[8,192,512]{2,1,0:T(8,128)(2,1)} %broadcast_in_dim.19), calls=%async_computation.6 | async-start | bytes 3145728 | tf_op jit(solution)/shard_map/all_to_all | solution.py:54
  316.3 140.4 %all-gather.16.cloned.1.call-start = ((), (), s32[]{:S(2)}) async-start(), calls=%async_computation.19 | async-start | bytes 1769472 | tf_op jit(solution)/shard_map/all_gather | solution.py:246
  316.9 329.8 %all-gather.22.cloned.1.call-start = ((), (), s32[]{:S(2)}) async-start(), calls=%async_computation.22 | async-start | bytes 6193152 | tf_op jit(solution)/shard_map/all_gather | solution.py:268
  354.8 17.7 %collective-permute-start.11 = (bf16[192,896]{1,0:T(8,128)(2,1)S(1)}, bf16[192,896]{1,0:T(8,128)(2,1)S(1)}, u32[]{:S(2)}, u32[]{:S(2)}) collective-permute-start(bf16[192,896]{1,0:T(8,128)(2,1)S(1)} %product_in.10), channel_id=1, source_target_pairs={{0,64},{64,0},{1,65},{65,1},{2,66},{66,2},{3,67},{67,3},{4,68},{68... | collective-permute-start | bytes 1032200 | tf_op jit(solution)/shard_map/ppermute | solution.py:32
  430.9 33.1 %all-to-all-start.9 = ((bf16[8,192,512]{2,1,0:T(8,128)(2,1)}), bf16[8,192,512]{2,1,0:T(8,128)(2,1)}, u32[]{:S(2)}, u32[]{:S(2)}) async-start(bf16[8,192,512]{2,1,0:T(8,128)(2,1)} %all-to-all-done.6.left), calls=%async_computation.9 | async-start | bytes 3145728 | tf_op jit(solution)/shard_map/all_to_all | solution.py:67
  443.2 212.7 %all-gather.18.cloned.1.call-start = ((), (), s32[]{:S(2)}) async-start(), calls=%async_computation.20 | async-start | bytes 6193152 | tf_op jit(solution)/shard_map/all_gather | solution.py:307
  449.1 16.8 %collective-permute-start.14 = (bf16[192,896]{1,0:T(8,128)(2,1)S(1)}, bf16[192,896]{1,0:T(8,128)(2,1)}, u32[]{:S(2)}, u32[]{:S(2)}) collective-permute-start(bf16[192,896]{1,0:T(8,128)(2,1)S(1)} %product_in.13), channel_id=1, source_target_pairs={{0,64},{64,0},{1,65},{65,1},{2,66},{66,2},{3,67},{67,3},{4,68},{68... | collective-permute-start | bytes 1032200 | tf_op jit(solution)/shard_map/ppermute | solution.py:32
  531.1 34.8 %all-to-all-start.12 = ((bf16[8,192,512]{2,1,0:T(8,128)(2,1)}), bf16[8,192,512]{2,1,0:T(8,128)(2,1)}, u32[]{:S(2)}, u32[]{:S(2)}) async-start(bf16[8,192,512]{2,1,0:T(8,128)(2,1)} %all_to_all.85.left), calls=%async_computation.12 | async-start | bytes 3145728 | tf_op jit(solution)/shard_map/all_to_all | solution.py:67
  538.8 125.2 %all-gather.20.cloned.1.call-start = ((), (), s32[]{:S(2)}) async-start(), calls=%async_computation.21 | async-start | bytes 6193152 | tf_op jit(solution)/shard_map/all_gather | solution.py:307
  549.3 16.5 %collective-permute-start.20 = (bf16[192,896]{1,0:T(8,128)(2,1)S(1)}, bf16[192,896]{1,0:T(8,128)(2,1)S(1)}, u32[]{:S(2)}, u32[]{:S(2)}) collective-permute-start(bf16[192,896]{1,0:T(8,128)(2,1)S(1)} %product_in.15), channel_id=1, source_target_pairs={{0,64},{64,0},{1,65},{65,1},{2,66},{66,2},{3,67},{67,3},{4,68},{68... | collective-permute-start | bytes 1032200 | tf_op jit(solution)/shard_map/ppermute | solution.py:32
  602.1 28.7 %all-to-all-start.14 = ((bf16[8,192,512]{2,1,0:T(8,128)(2,1)}), bf16[8,192,512]{2,1,0:T(8,128)(2,1)S(1)}, u32[]{:S(2)}, u32[]{:S(2)}) async-start(bf16[8,192,512]{2,1,0:T(8,128)(2,1)} %all_to_all.83.left), calls=%async_computation.14 | async-start | bytes 3145728 | tf_op jit(solution)/shard_map/all_to_all | solution.py:67
  635.2 38.0 %all-to-all-start.15 = ((bf16[8,192,512]{2,1,0:T(8,128)(2,1)}), bf16[8,192,512]{2,1,0:T(8,128)(2,1)S(1)}, u32[]{:S(2)}, u32[]{:S(2)}) async-start(bf16[8,192,512]{2,1,0:T(8,128)(2,1)} %broadcast_in_dim.23), calls=%async_computation.15 | async-start | bytes 3145728 | tf_op jit(solution)/shard_map/all_to_all | solution.py:54
  (52 other events, 685.5 us)
Sparse Core Ops, SparseCore 0:
  9.7 39.7 all-gather.9
  51.8 109.6 all-gather.11
  163.1 85.9 all-gather.23
  271.7 38.2 all-gather.13
  319.1 60.9 all-gather.15
  382.2 39.5 all-gather.21
  469.8 35.0 all-gather.17
  569.4 37.6 all-gather.19

commit v3 on v2

--- a/solution.py
+++ b/solution.py
@@ -268,7 +268,7 @@
         active_all = lax.all_gather(active, "tensor", axis=0, tiled=True)
         saved.append((xfull, scale, inner, active_all, error))
         state = following
-    scaled_all, sources = [], []
+    scaled_all = []
     rate = 1.0 / math.sqrt(tokens)
     grad = jnp.zeros((rows, width), F32)
     grad_inner = jnp.zeros(inner_weight.shape, F32)
@@ -280,8 +280,7 @@
         grad_all = copies(grad_half, "dp", n_dp)
         grad_tokens = to_feature_owners(grad_all)
         back_act = jnp.concatenate(summed_in(grad_all, outer_all, True), axis=1)
-        if step == 0:
-            back_act = after(back_act, grad_tokens)
+        back_act = after(back_act, grad_tokens)
         if step < STEPS - 1:
             back_act = after(back_act, mean_error)
         else:
@@ -299,9 +298,8 @@
             total_dp = jnp.broadcast_to(moved[rows], (128,))
         moved = moved[:rows, None]
         grad = grad + scale * back_norm - xfull * scale**2 * moved / D
-        sources.append((active_all, grad_tokens))
+        grad_outer = grad_outer + contract_rows(active_all, grad_tokens)
         if step == 0:
-            grad_outer = contract_rows(active_all, grad_tokens)
             grad = after(grad, grad_outer)
         scaled = (scale * grad_in_wide).astype(BF16)
         scaled_all.append(lax.all_gather(scaled, "tensor", axis=0, tiled=True))
@@ -311,13 +309,11 @@
                     total_dp, "tensor", [(i, i ^ k) for i in range(n_tensor)]
                 )
             mean_error = (total_dp + other_group(total_dp))[0] / (STEPS * tokens * D)
-    swapped = after(swap_axes(grad.astype(BF16)), *[source[1] for source in sources])
-    for units, features in sources[:-1]:
-        grad_outer = grad_outer + contract_rows(units, features)
+    swapped = after(swap_axes(grad.astype(BF16)), *x_tokens)
     for step, units in zip(reversed(range(STEPS)), scaled_all):
         grad_inner = grad_inner + gain * contract_rows(x_tokens[step], units)
     grad_tokens = copies(swapped, "dp", n_dp).reshape(tokens, width)
-    grad_tokens = after(grad_tokens, grad_inner, grad_outer)
+    grad_tokens = after(grad_tokens, grad_inner)
     grad_join = jnp.stack([contract_rows(source, grad_tokens) for source in hidden_all])
     return (mean_error, grad_join, grad_inner, grad_outer)
 

time: 699 us -> 708 us (1.013)
  waiting for transfers between devices: 195 us -> 224 us
  blocking collectives: 187 us -> 168 us
    all_to_all x4 -> x3, blocking collectives: 101 us -> 77.8 us  [total_of(): lax.all_to_all(blocks, axis, 0, 0, tiled=True, axis_index_groups=groups)]
    all_to_all x2 -> x3, waiting for transfers between devices: 27.9 us -> 38.6 us  [total_of(): lax.all_to_all(blocks, axis, 0, 0, tiled=True, axis_index_groups=groups)]
  transfers between devices with their start and end apart: 39 -> 40, of which waited for: 18 -> 21; matrix products, arithmetic and copies ran while one was open for 13% -> 13% of each run, Pallas kernels for 11% -> 11%
where the time goes in v3:
time: 708 us; the launch traced here: 701 us
  waiting for transfers between devices  224 us (32%)
  blocking collectives  168 us (24%)
  starting transfers between devices  94.4 us (13%)
  Pallas kernels  78 us (11%)
  other arithmetic  38.9 us (5%)
  matrix products  38.6 us (5%)
  local copies, waits for them, and re-layouts  34.4 us (5%)
  between operations  24.2 us (3%)
    all_to_all x3, blocking collectives, copies(): lax.all_to_all(sent, axis, 0, 0, tiled=True, axis_index_groups=groups)  90.6 us
    all_to_all x3, blocking collectives, total_of(): lax.all_to_all(blocks, axis, 0, 0, tiled=True, axis_index_groups=groups)  77.8 us
    all_to_all x4, waiting for transfers between devices, copies(): lax.all_to_all(sent, axis, 0, 0, tiled=True, axis_index_groups=groups)  58.8 us
    pallas_call x8, Pallas kernels, product_in(): pl.pallas_call(functools.partial(blocks_in_kernel, flipped), grid=(n // e...  44.8 us
    all_to_all x3, waiting for transfers between devices, total_of(): lax.all_to_all(blocks, axis, 0, 0, tiled=True, axis_index_groups=groups)  38.6 us
    ppermute x3, waiting for transfers between devices, swap_axes(): return lax.ppermute(values, EVERY, route)  36.4 us
    ppermute x1, waiting for transfers between devices, shifted(): return lax.ppermute(block, axis, route)  34.8 us
    pallas_call x4, Pallas kernels, product_out(): pl.pallas_call(functools.partial(blocks_out_kernel, flipped), grid=(n //...  33.2 us
  transfers between devices with their start and end apart: 40, of which 21 were waited for; matrix products, arithmetic and copies ran while one was open for 13% of the time, Pallas kernels for 11%

profile of v3, /device:TPU:1, one launch (start us, length us, event | category | flops | bytes accessed | tf_op | source)
XLA Modules:
  0.0 701.2 jit_solution(7488057180064715540)
XLA Ops:
  14.5 8.5 %all-to-all-start = ((bf16[8,192,512]{2,1,0:T(8,128)(2,1)}), bf16[8,192,512]{2,1,0:T(8,128)(2,1)S(1)}, u32[]{:S(2)}, u32[]{:S(2)}) async-start(bf16[8,192,512]{2,1,0:T(8,128)(2,1)} %broadcast_in_dim.16), calls=%async_computation | async-start | bytes 3145728 | tf_op jit(solution)/shard_map/all_to_all | solution.py:54
  27.5 25.6 %collective-permute-done.2 = bf16[192,512]{1,0:T(8,128)(2,1)S(1)} collective-permute-done((bf16[192,512]{1,0:T(8,128)(2,1)S(1)}, bf16[192,512]{1,0:T(8,128)(2,1)S(1)}, u32[]{:S(2)}, u32[]{:S(2)}) %collective-permute-start.2) | collective-permute-done | bytes 196640 | tf_op jit(solution)/shard_map/ppermute | solution.py:43
  71.2 34.8 %collective-permute-done.3 = bf16[3,512]{1,0:T(4,128)(2,1)S(1)} collective-permute-done((bf16[3,512]{1,0:T(4,128)(2,1)S(1)}, bf16[3,512]{1,0:T(4,128)(2,1)S(1)}, u32[]{:S(2)}, u32[]{:S(2)}) %collective-permute-start.3) | collective-permute-done | bytes 3104 | tf_op jit(solution)/shard_map/ppermute | solution.py:49
  124.8 30.9 %all-to-all-done.2 = bf16[8,96,1024]{2,1,0:T(8,128)(2,1)} async-done(((bf16[8,96,1024]{2,1,0:T(8,128)(2,1)}), bf16[8,96,1024]{2,1,0:T(8,128)(2,1)}, u32[]{:S(2)}, u32[]{:S(2)}) %all-to-all-start.2) | async-done | bytes 1572896 | tf_op jit(solution)/shard_map/all_to_all | solution.py:54
  171.4 29.3 %all_to_all.80 = bf16[8,192,512]{2,1,0:T(8,128)(2,1)S(1)} all-to-all(bf16[8,192,512]{2,1,0:T(8,128)(2,1)S(1)} %bitcast.93), channel_id=1, replica_groups=mesh['group'=2,'dp'=8,'tensor'=8] {'dp'}, dimensions={0} | all-to-all | bytes 3145728 | tf_op jit(solution)/shard_map/all_to_all | solution.py:58
  208.5 39.9 %all_to_all.81.left = bf16[8,192,512]{2,1,0:T(8,128)(2,1)S(1)} all-to-all(bf16[8,192,512]{2,1,0:T(8,128)(2,1)S(1)} %broadcast_in_dim.18), channel_id=1, replica_groups=mesh['group'=2,'dp'=8,'tensor'=8] {'dp'}, dimensions={0} | all-to-all | bytes 3145728 | tf_op jit(solution)/shard_map/all_to_all | solution.py:54
  261.9 8.3 %collective-permute-done.8 = bf16[192,896]{1,0:T(8,128)(2,1)S(1)} collective-permute-done((bf16[192,896]{1,0:T(8,128)(2,1)S(1)}, bf16[192,896]{1,0:T(8,128)(2,1)S(1)}, u32[]{:S(2)}, u32[]{:S(2)}) %collective-permute-start.8) | collective-permute-done | bytes 344096 | tf_op jit(solution)/shard_map/ppermute | solution.py:32
  272.6 8.1 %product_out.4 = bf16[8,192,512]{2,1,0:T(8,128)(2,1)} custom-call(bf16[192,1792]{1,0:T(8,128)(2,1)S(1)} %copy-done.3, bf16[8,1792,512]{2,1,0:T(8,128)(2,1)} %bitcast.80), custom_call_target="tpu_custom_call" | custom-call | flops 2818572288 | bytes 16252928 | tf_op jit(solution)/shard_map/product_out/pallas_call | solution.py:136
  285.5 22.7 %all-to-all-done.5 = bf16[8,192,512]{2,1,0:T(8,128)(2,1)} async-done(((bf16[8,192,512]{2,1,0:T(8,128)(2,1)}), bf16[8,192,512]{2,1,0:T(8,128)(2,1)}, u32[]{:S(2)}, u32[]{:S(2)}) %all-to-all-start.5) | async-done | bytes 1572896 | tf_op jit(solution)/shard_map/all_to_all | solution.py:58
  316.9 22.3 %all-to-all-done.6.left = bf16[8,192,512]{2,1,0:T(8,128)(2,1)} async-done(((bf16[8,192,512]{2,1,0:T(8,128)(2,1)}), bf16[8,192,512]{2,1,0:T(8,128)(2,1)}, u32[]{:S(2)}, u32[]{:S(2)}) %all-to-all-start.6) | async-done | bytes 1572896 | tf_op jit(solution)/shard_map/all_to_all | solution.py:54
  357.6 14.8 %collective-permute-done.11 = bf16[192,896]{1,0:T(8,128)(2,1)S(1)} collective-permute-done((bf16[192,896]{1,0:T(8,128)(2,1)S(1)}, bf16[192,896]{1,0:T(8,128)(2,1)S(1)}, u32[]{:S(2)}, u32[]{:S(2)}) %collective-permute-start.11) | collective-permute-done | bytes 344096 | tf_op jit(solution)/shard_map/ppermute | solution.py:32
  376.8 7.2 %product_out.5 = bf16[8,192,512]{2,1,0:T(8,128)(2,1)S(1)} custom-call(bf16[192,1792]{1,0:T(8,128)(2,1)S(1)} %copy-done.2, bf16[8,1792,512]{2,1,0:T(8,128)(2,1)} %bitcast.81), custom_call_target="tpu_custom_call" | custom-call | flops 2818572288 | bytes 16252928 | tf_op jit(solution)/shard_map/product_out/pallas_call | solution.py:136
  384.0 23.3 %all_to_all.82 = bf16[8,192,512]{2,1,0:T(8,128)(2,1)} all-to-all(bf16[8,192,512]{2,1,0:T(8,128)(2,1)S(1)} %product_out.5), channel_id=1, replica_groups=mesh['group'=2,'dp'=8,'tensor'=8] {'dp'}, dimensions={0} | all-to-all | bytes 3145728 | tf_op jit(solution)/shard_map/all_to_all | solution.py:58
  407.3 10.2 %all-to-all-start.10 = ((bf16[8,192,512]{2,1,0:T(8,128)(2,1)}), bf16[8,192,512]{2,1,0:T(8,128)(2,1)}, u32[]{:S(2)}, u32[]{:S(2)}) async-start(bf16[8,192,512]{2,1,0:T(8,128)(2,1)} %all-to-all-done.6.left), calls=%async_computation.10 | async-start | bytes 3145728 | tf_op jit(solution)/shard_map/all_to_all | solution.py:67
  420.8 17.6 %all-to-all-done.10 = bf16[8,192,512]{2,1,0:T(8,128)(2,1)} async-done(((bf16[8,192,512]{2,1,0:T(8,128)(2,1)}), bf16[8,192,512]{2,1,0:T(8,128)(2,1)}, u32[]{:S(2)}, u32[]{:S(2)}) %all-to-all-start.10) | async-done | bytes 1572896 | tf_op jit(solution)/shard_map/all_to_all | solution.py:67
  438.5 27.2 %all_to_all.83.left = bf16[8,192,512]{2,1,0:T(8,128)(2,1)} all-to-all(bf16[8,192,512]{2,1,0:T(8,128)(2,1)S(1)} %broadcast_in_dim.20), channel_id=1, replica_groups=mesh['group'=2,'dp'=8,'tensor'=8] {'dp'}, dimensions={0} | all-to-all | bytes 3145728 | tf_op jit(solution)/shard_map/all_to_all | solution.py:54
  503.0 8.6 %product_out.6 = bf16[8,208,512]{2,1,0:T(8,128)(2,1)S(1)} custom-call(bf16[192,1792]{1,0:T(8,128)(2,1)S(1)} %get-tuple-element.7.left, bf16[8,512,1792]{2,1,0:T(8,128)(2,1)} %bitcast.78, bf16[16,512]{1,0:T(8,128)(2,1)S(1)} %fusion.47.rest_0_), custom_call_target="tpu_custom_call" | custom-call | flops 2818572288 | bytes 16252928 | tf_op jit(solution)/shard_map/product_out/pallas_call | solution.py:136
  511.6 25.2 %all_to_all.84 = bf16[8,208,512]{2,1,0:T(8,128)(2,1)S(1)} all-to-all(bf16[8,208,512]{2,1,0:T(8,128)(2,1)S(1)} %product_out.6), channel_id=1, replica_groups=mesh['group'=2,'dp'=8,'tensor'=8] {'dp'}, dimensions={0} | all-to-all | bytes 3407872 | tf_op jit(solution)/shard_map/all_to_all | solution.py:58
  539.1 23.5 %all_to_all.85.left = bf16[8,192,512]{2,1,0:T(8,128)(2,1)} all-to-all(bf16[8,192,512]{2,1,0:T(8,128)(2,1)S(1)} %broadcast_in_dim.22), channel_id=1, replica_groups=mesh['group'=2,'dp'=8,'tensor'=8] {'dp'}, dimensions={0} | all-to-all | bytes 3145728 | tf_op jit(solution)/shard_map/all_to_all | solution.py:54
  562.6 7.6 %all-to-all-start.13 = ((bf16[8,192,512]{2,1,0:T(8,128)(2,1)}), bf16[8,192,512]{2,1,0:T(8,128)(2,1)}, u32[]{:S(2)}, u32[]{:S(2)}) async-start(bf16[8,192,512]{2,1,0:T(8,128)(2,1)} %all_to_all.85.left), calls=%async_computation.13 | async-start | bytes 3145728 | tf_op jit(solution)/shard_map/all_to_all | solution.py:67
  601.4 9.2 %product_out.7 = bf16[8,208,512]{2,1,0:T(8,128)(2,1)} custom-call(bf16[192,1792]{1,0:T(8,128)(2,1)S(1)} %get-tuple-element.5.left, bf16[8,512,1792]{2,1,0:T(8,128)(2,1)} %bitcast.79, bf16[16,512]{1,0:T(8,128)(2,1)S(1)} %fusion.52.rest_0_), custom_call_target="tpu_custom_call" | custom-call | flops 2818572288 | bytes 16252928 | tf_op jit(solution)/shard_map/product_out/pallas_call | solution.py:136
  627.8 10.7 %all-to-all-done.14 = bf16[8,208,512]{2,1,0:T(8,128)(2,1)S(1)} async-done(((bf16[8,208,512]{2,1,0:T(8,128)(2,1)}), bf16[8,208,512]{2,1,0:T(8,128)(2,1)S(1)}, u32[]{:S(2)}, u32[]{:S(2)}) %all-to-all-start.14) | async-done | bytes 1703968 | tf_op jit(solution)/shard_map/all_to_all | solution.py:58
  650.2 9.0 %all-to-all-start.15 = ((bf16[8,192,512]{2,1,0:T(8,128)(2,1)}), bf16[8,192,512]{2,1,0:T(8,128)(2,1)S(1)}, u32[]{:S(2)}, u32[]{:S(2)}) async-start(bf16[8,192,512]{2,1,0:T(8,128)(2,1)} %broadcast_in_dim.23), calls=%async_computation.15 | async-start | bytes 3145728 | tf_op jit(solution)/shard_map/all_to_all | solution.py:54
  659.2 8.0 %fusion.75 = f32[512,1792]{1,0:T(8,128)} fusion(bf16[1536,512]{1,0:T(8,128)(2,1)} %bitcast.24, bf16[1536,1792]{1,0:T(8,128)(2,1)} %all-gather.20.cloned.1.call-done), kind=kOutput, calls=%fused_computation.148 | convolution fusion | flops 2818572288 | bytes 10747904 | tf_op jit(solution)/shard_map/dot_general | solution.py:63
  (245 shorter events, 244.4 us)
Async XLA Ops:
  7.2 51.1 %all-gather.10.cloned.1.call-start = ((), (), s32[]{:S(2)}) async-start(), calls=%async_computation.16 | async-start | bytes 3538944 | tf_op jit(solution)/shard_map/all_gather | solution.py:208
  9.1 240.4 %all-gather.12.cloned.1.call-start = ((), (), s32[]{:S(2)}) async-start(), calls=%async_computation.17 | async-start | bytes 16515072 | tf_op jit(solution)/shard_map/all_gather | solution.py:222
  12.3 259.2 %all-gather.24.cloned.1.call-start = ((), (), s32[]{:S(2)}) async-start(), calls=%async_computation.23 | async-start | bytes 16515072 | tf_op jit(solution)/shard_map/all_gather | solution.py:224
  14.5 39.7 %all-to-all-start = ((bf16[8,192,512]{2,1,0:T(8,128)(2,1)}), bf16[8,192,512]{2,1,0:T(8,128)(2,1)S(1)}, u32[]{:S(2)}, u32[]{:S(2)}) async-start(bf16[8,192,512]{2,1,0:T(8,128)(2,1)} %broadcast_in_dim.16), calls=%async_computation | async-start | bytes 3145728 | tf_op jit(solution)/shard_map/all_to_all | solution.py:54
  23.0 30.1 %collective-permute-start.2 = (bf16[192,512]{1,0:T(8,128)(2,1)S(1)}, bf16[192,512]{1,0:T(8,128)(2,1)S(1)}, u32[]{:S(2)}, u32[]{:S(2)}) collective-permute-start(bf16[192,512]{1,0:T(8,128)(2,1)S(1)} %copy-done.34), channel_id=1, source_target_pairs={{0,0},{1,8},{2,16},{3,24},{4,32},{5,40},{6,48},{7,56},{8,1},{9,9},... | collective-permute-start | bytes 589832 | tf_op jit(solution)/shard_map/ppermute | solution.py:43
  59.9 52.8 %collective-permute-start = (bf16[4,96,2048]{2,1,0:T(8,128)(2,1)S(1)}, bf16[4,96,2048]{2,1,0:T(8,128)(2,1)}, u32[]{:S(2)}, u32[]{:S(2)}) collective-permute-start(bf16[4,96,2048]{2,1,0:T(8,128)(2,1)S(1)} %dynamic-slice_bitcast_fusion.1), channel_id=1, source_target_pairs={{0,64},{64,0},{1,65},{65,1},{2,66},{66,2},{3,67},{67,3},{4,68},{68... | collective-permute-start | bytes 4718600 | tf_op jit(solution)/shard_map/ppermute | solution.py:32
  63.7 48.7 %all-to-all-start.1 = ((bf16[8,96,1024]{2,1,0:T(8,128)(2,1)}), bf16[8,96,1024]{2,1,0:T(8,128)(2,1)S(1)}, u32[]{:S(2)}, u32[]{:S(2)}) async-start(bf16[8,96,1024]{2,1,0:T(8,128)(2,1)} %fusion), calls=%async_computation.1 | async-start | bytes 3145728 | tf_op jit(solution)/shard_map/all_to_all | solution.py:58
  68.5 37.5 %collective-permute-start.3 = (bf16[3,512]{1,0:T(4,128)(2,1)S(1)}, bf16[3,512]{1,0:T(4,128)(2,1)S(1)}, u32[]{:S(2)}, u32[]{:S(2)}) collective-permute-start(bf16[3,512]{1,0:T(4,128)(2,1)S(1)} %slice.157), channel_id=1, source_target_pairs={{1,0},{2,1},{3,2},{4,3},{5,4},{6,5},{7,6},{9,8},{10,9},{11,10},{12... | collective-permute-start | bytes 9224 | tf_op jit(solution)/shard_map/ppermute | solution.py:49
  114.5 41.9 %collective-permute-start.1 = (bf16[4,96,2048]{2,1,0:T(8,128)(2,1)}, bf16[4,96,2048]{2,1,0:T(8,128)(2,1)}, u32[]{:S(2)}, u32[]{:S(2)}) collective-permute-start(bf16[4,96,2048]{2,1,0:T(8,128)(2,1)} %collective-permute-done), channel_id=1, source_target_pairs={{0,1},{1,0},{2,3},{3,2},{4,5},{5,4},{6,7},{7,6},{8,9},{9,8},{10,11... | collective-permute-start | bytes 4718600 | tf_op jit(solution)/shard_map/ppermute | solution.py:28
  117.3 38.4 %all-to-all-start.2 = ((bf16[8,96,1024]{2,1,0:T(8,128)(2,1)}), bf16[8,96,1024]{2,1,0:T(8,128)(2,1)}, u32[]{:S(2)}, u32[]{:S(2)}) async-start(bf16[8,96,1024]{2,1,0:T(8,128)(2,1)} %broadcast_in_dim.17), calls=%async_computation.2 | async-start | bytes 3145728 | tf_op jit(solution)/shard_map/all_to_all | solution.py:54
  122.7 249.8 %all-gather.14.cloned.1.call-start = ((), (), s32[]{:S(2)}) async-start(), calls=%async_computation.18 | async-start | bytes 6193152 | tf_op jit(solution)/shard_map/all_gather | solution.py:268
  280.8 27.4 %all-to-all-start.5 = ((bf16[8,192,512]{2,1,0:T(8,128)(2,1)}), bf16[8,192,512]{2,1,0:T(8,128)(2,1)}, u32[]{:S(2)}, u32[]{:S(2)}) async-start(bf16[8,192,512]{2,1,0:T(8,128)(2,1)} %product_out.4), calls=%async_computation.5 | async-start | bytes 3145728 | tf_op jit(solution)/shard_map/all_to_all | solution.py:58
  312.0 27.3 %all-to-all-start.6 = ((bf16[8,192,512]{2,1,0:T(8,128)(2,1)}), bf16[8,192,512]{2,1,0:T(8,128)(2,1)}, u32[]{:S(2)}, u32[]{:S(2)}) async-start(bf16[8,192,512]{2,1,0:T(8,128)(2,1)} %broadcast_in_dim.19), calls=%async_computation.6 | async-start | bytes 3145728 | tf_op jit(solution)/shard_map/all_to_all | solution.py:54
  316.3 168.8 %all-gather.16.cloned.1.call-start = ((), (), s32[]{:S(2)}) async-start(), calls=%async_computation.19 | async-start | bytes 1769472 | tf_op jit(solution)/shard_map/all_gather | solution.py:246
  316.8 297.4 %all-gather.18.cloned.1.call-start = ((), (), s32[]{:S(2)}) async-start(), calls=%async_computation.20 | async-start | bytes 6193152 | tf_op jit(solution)/shard_map/all_gather | solution.py:268
  354.7 17.7 %collective-permute-start.11 = (bf16[192,896]{1,0:T(8,128)(2,1)S(1)}, bf16[192,896]{1,0:T(8,128)(2,1)S(1)}, u32[]{:S(2)}, u32[]{:S(2)}) collective-permute-start(bf16[192,896]{1,0:T(8,128)(2,1)S(1)} %product_in.10), channel_id=1, source_target_pairs={{0,64},{64,0},{1,65},{65,1},{2,66},{66,2},{3,67},{67,3},{4,68},{68... | collective-permute-start | bytes 1032200 | tf_op jit(solution)/shard_map/ppermute | solution.py:32
  407.3 31.0 %all-to-all-start.10 = ((bf16[8,192,512]{2,1,0:T(8,128)(2,1)}), bf16[8,192,512]{2,1,0:T(8,128)(2,1)}, u32[]{:S(2)}, u32[]{:S(2)}) async-start(bf16[8,192,512]{2,1,0:T(8,128)(2,1)} %all-to-all-done.6.left), calls=%async_computation.10 | async-start | bytes 3145728 | tf_op jit(solution)/shard_map/all_to_all | solution.py:67
  465.6 30.8 %all-to-all-start.9 = ((bf16[8,192,512]{2,1,0:T(8,128)(2,1)}), bf16[8,192,512]{2,1,0:T(8,128)(2,1)}, u32[]{:S(2)}, u32[]{:S(2)}) async-start(bf16[8,192,512]{2,1,0:T(8,128)(2,1)} %all_to_all.83.left), calls=%async_computation.9 | async-start | bytes 3145728 | tf_op jit(solution)/shard_map/all_to_all | solution.py:67
  471.6 187.6 %all-gather.20.cloned.1.call-start = ((), (), s32[]{:S(2)}) async-start(), calls=%async_computation.21 | async-start | bytes 6193152 | tf_op jit(solution)/shard_map/all_gather | solution.py:305
  562.6 34.9 %all-to-all-start.13 = ((bf16[8,192,512]{2,1,0:T(8,128)(2,1)}), bf16[8,192,512]{2,1,0:T(8,128)(2,1)}, u32[]{:S(2)}, u32[]{:S(2)}) async-start(bf16[8,192,512]{2,1,0:T(8,128)(2,1)} %all_to_all.85.left), calls=%async_computation.13 | async-start | bytes 3145728 | tf_op jit(solution)/shard_map/all_to_all | solution.py:67
  570.2 97.0 %all-gather.22.cloned.1.call-start = ((), (), s32[]{:S(2)}) async-start(), calls=%async_computation.22 | async-start | bytes 6193152 | tf_op jit(solution)/shard_map/all_gather | solution.py:305
  580.7 16.6 %collective-permute-start.20 = (bf16[192,896]{1,0:T(8,128)(2,1)S(1)}, bf16[192,896]{1,0:T(8,128)(2,1)S(1)}, u32[]{:S(2)}, u32[]{:S(2)}) collective-permute-start(bf16[192,896]{1,0:T(8,128)(2,1)S(1)} %product_in.15), channel_id=1, source_target_pairs={{0,64},{64,0},{1,65},{65,1},{2,66},{66,2},{3,67},{67,3},{4,68},{68... | collective-permute-start | bytes 1032200 | tf_op jit(solution)/shard_map/ppermute | solution.py:32
  610.6 27.9 %all-to-all-start.14 = ((bf16[8,208,512]{2,1,0:T(8,128)(2,1)}), bf16[8,208,512]{2,1,0:T(8,128)(2,1)S(1)}, u32[]{:S(2)}, u32[]{:S(2)}) async-start(bf16[8,208,512]{2,1,0:T(8,128)(2,1)} %product_out.7), calls=%async_computation.14 | async-start | bytes 3407872 | tf_op jit(solution)/shard_map/all_to_all | solution.py:58
  650.2 31.9 %all-to-all-start.15 = ((bf16[8,192,512]{2,1,0:T(8,128)(2,1)}), bf16[8,192,512]{2,1,0:T(8,128)(2,1)S(1)}, u32[]{:S(2)}, u32[]{:S(2)}) async-start(bf16[8,192,512]{2,1,0:T(8,128)(2,1)} %broadcast_in_dim.23), calls=%async_computation.15 | async-start | bytes 3145728 | tf_op jit(solution)/shard_map/all_to_all | solution.py:54
  (52 other events, 737.3 us)
Sparse Core Ops, SparseCore 0:
  9.7 39.7 all-gather.9
  51.8 109.6 all-gather.11
  163.1 85.9 all-gather.23
  271.6 38.2 all-gather.13
  319.1 60.9 all-gather.15
  382.2 39.5 all-gather.17
  501.4 35.9 all-gather.19
  601.1 36.6 all-gather.21
